TPU v7x, 32 devices: a whole 2x2x4 slice. The times are simulated.
32 devices in a mesh: lon: 16 (over z, x, core), lat: 2 (over y).
Axes of the slice: x: 2, y: 2, z: 4, core: 2. Of those that a mesh axis runs over, the one named last changes fastest.
Arguments:
- state: float32 [3, 256, 16, 4096], P(None, None, 'lat', 'lon'), may hold values from -6 to 6
- bathymetry: float32 [16, 4096], P('lat', 'lon'), may hold values from 0.5 to 2
- obs_index: int32 [2, 16, 256], P('lat', 'lon'), may hold values from 0 to 2047
- obs_count: int32 [2, 16], P('lat', 'lon'), may hold values from 85 to 256, as said below
- obs_value: float32 [2, 16, 256], P('lat', 'lon'), may hold values from -6 to 6
- obs_sd: float32 [2, 16, 256], P('lat', 'lon'), may hold values from 0.5 to 2
Outputs:
- analysis: float32 [3, 256, 16, 4096], P(None, None, 'lat', 'lon')
Inputs may be any that keep to these rules, and one draw needn't show every extreme that they name: `obs_count`: at least 85 slots of every tile are used; at least one tile uses all 256. `obs_index`: several slots may name the same cell.
All inputs are finite; a program needn't handle non-finite values.
Results may differ from a plain program's by a relative error of at most 0.000051.
Values sent between devices are 32-bit elements; how exact they have to be, the bound alone decides.
A program may use at most 128 MiB of HBM per device.

v0:
```python
import math

import jax
import jax.numpy as jnp
from jax import lax
from jax.sharding import PartitionSpec as P


def with_halo(value, sides, width, wrap):
    for axis, dim in sides:
        count, length = (lax.axis_size(axis), value.shape[dim])
        up = [(i, (i + 1) % count) for i in range(count if wrap else count - 1)]
        down = [(j, i) for i, j in up]
        last = lax.slice_in_dim(value, length - width, length, axis=dim)
        first = lax.slice_in_dim(value, 0, width, axis=dim)
        before = lax.ppermute(last, axis, up)
        after = lax.ppermute(first, axis, down)
        value = jnp.concatenate([before, value, after], axis=dim)
    return value


def coriolis(rows, total):
    return jnp.sin(math.pi / 3.0 * ((rows.astype(jnp.float32) + 0.5) / total - 0.5))[:, None]


def extend(field, width):
    wide = with_halo(field, (("lat", 2),), width, False)
    return with_halo(wide, (("lon", 3),), width, True)


def new_height(height, flux, keep):
    div = (
        flux[0][:, 1:-1, 2:] - flux[0][:, 1:-1, :-2] + flux[1][:, 2:, 1:-1] - flux[1][:, :-2, 1:-1]
    )
    return (height - 0.25 * div) * keep


def new_wind(east, north, height, fcor, keep):
    grad_x = height[:, 1:-1, 2:] - height[:, 1:-1, :-2]
    grad_y = height[:, 2:, 1:-1] - height[:, :-2, 1:-1]
    east_new = (east + 0.5 * (fcor * north - 0.5 * grad_x)) * keep
    north_new = (north - 0.5 * (fcor * east + 0.5 * grad_y)) * keep
    return (east_new, north_new)


def shards(state, bathymetry, obs_index, obs_count, obs_value, obs_sd):
    members, nrows, ncols = (state.shape[1], state.shape[2], state.shape[3])
    total_rows = nrows * lax.axis_size("lat")
    base = lax.axis_index("lat") * nrows
    fcor = coriolis(base + jnp.arange(nrows), total_rows)
    height, east, north = (state[0], state[1], state[2])
    for step in range(2):
        flux = extend(jnp.stack([bathymetry * east, bathymetry * north]), 1)
        height = new_height(height, flux, 1.0)
        tall = extend(height[None], 1)[0]
        east, north = new_wind(east, north, tall, fcor, 1.0)
    slots = obs_index.shape[2]
    flat_height = height.reshape(members, nrows * ncols)
    hx = jnp.take(flat_height, obs_index.reshape(-1), axis=1)
    valid = (jnp.arange(slots) < obs_count.reshape(())).astype(jnp.float32)
    sigma = obs_sd.reshape(-1) * (
        math.sqrt(slots * lax.axis_size("lat") * lax.axis_size("lon")) / 16.0
    )
    hmean = jnp.mean(hx, axis=0)
    anomal = (hx - hmean) / (math.sqrt(members - 1) * sigma) * valid
    innov = (obs_value.reshape(-1) - hmean) / sigma * valid
    gram = jnp.dot(anomal, anomal.T, precision=lax.Precision.HIGHEST)
    proj = jnp.dot(anomal, innov, precision=lax.Precision.HIGHEST)
    gram, proj = lax.psum((gram, proj), ("lon", "lat"))
    eye = jnp.eye(members, dtype=jnp.float32)
    lower = jnp.linalg.cholesky(gram + eye)
    inv_lower = jax.scipy.linalg.solve_triangular(lower, eye, lower=True)
    weights = jax.scipy.linalg.cho_solve((lower, True), proj)
    transform = inv_lower.T + weights[:, None] / math.sqrt(members - 1)
    fields = jnp.stack([height, east, north])
    center = jnp.mean(fields, axis=1, keepdims=True)
    mixed = jnp.einsum("nm,cnab->cmab", transform, fields - center, precision=lax.Precision.HIGHEST)
    return center + mixed


def solution(mesh):
    return jax.shard_map(
        shards,
        mesh=mesh,
        in_specs=(
            P(None, None, "lat", "lon"),
            P("lat", "lon"),
            P("lat", "lon", None),
            P("lat", "lon"),
            P("lat", "lon", None),
            P("lat", "lon", None),
        ),
        out_specs=P(None, None, "lat", "lon"),
        check_vma=False,
    )
```

profile of v0, /device:TPU:0, one launch (start us, length us, event | category | flops | bytes accessed | tf_op | source)
XLA Modules:
  0.0 364.5 jit_solution(13144336994013887668)
XLA Ops:
  6.5 5.7 %fusion.62 = (f32[1,256,8,256]{3,2,1,0:T(8,128)}, f32[1,256,8,256]{3,2,1,0:T(8,128)}, f32[1,256,8,256]{3,2,1,0:T(8,128)}) fusion(f32[3,256,8,256]{3,2,1,0:T(8,128)} %param.6), kind=kLoop, calls=%fused_computation.140 | loop fusion | bytes 12582912 | tf_op jit(solution)/shard_map/slice | solution.py:51
  12.2 1.9 copy.68
  14.2 1.3 copy-done.4
  15.9 2.2 copy.43
  18.0 4.2 %copy.66 = f32[1,256,8,256]{1,0,3,2:T(1,128)} copy(f32[1,256,8,256]{3,2,1,0:T(8,128)} %get-tuple-element.32) | data formatting | bytes 4194304
  22.2 4.0 %broadcast_multiply_fusion = f32[1,256,8,256]{1,0,3,2:T(1,128)S(1)} fusion(f32[1,256,8,256]{1,0,3,2:T(1,128)} %copy.66, f32[8,256]{1,0:T(8,128)S(1)} %copy-done.12), kind=kLoop, calls=%fused_computation.67 | loop fusion | flops 524288 | bytes 4202496 | tf_op jit(solution)/shard_map/mul | solution.py:53
  26.3 0.9 pad_maximum_fusion.11
  27.2 4.9 %collective-permute-start = (f32[2,256,1,256]{1,0,3,2:T(2,128)S(1)}, f32[2,256,1,256]{1,0,3,2:T(2,128)S(1)}, u32[]{:S(2)}, u32[]{:S(2)}) collective-permute-start(f32[2,256,1,256]{1,0,3,2:T(2,128)S(1)} %get-tuple-element.44), channel_id=1, source_target_pairs={{0,1},{2,3},{4,5},{6,7},{8,9},{10,11},{12,13},{14,15},{16,17},{18,... | collective-permute-start | bytes 1572872 | tf_op jit(solution)/shard_map/ppermute | solution.py:16
  32.1 1.3 collective-permute-start.1
  33.4 9.8 %collective-permute-done = f32[2,256,1,256]{1,0,3,2:T(2,128)S(1)} collective-permute-done((f32[2,256,1,256]{1,0,3,2:T(2,128)S(1)}, f32[2,256,1,256]{1,0,3,2:T(2,128)S(1)}, u32[]{:S(2)}, u32[]{:S(2)}) %collective-permute-start) | collective-permute-done | bytes 524320 | tf_op jit(solution)/shard_map/ppermute | solution.py:16
  43.3 4.1 %collective-permute-done.1 = f32[2,256,1,256]{1,0,3,2:T(2,128)S(1)} collective-permute-done((f32[2,256,1,256]{1,0,3,2:T(2,128)S(1)}, f32[2,256,1,256]{1,0,3,2:T(2,128)S(1)}, u32[]{:S(2)}, u32[]{:S(2)}) %collective-permute-start.1) | collective-permute-done | bytes 524320 | tf_op jit(solution)/shard_map/ppermute | solution.py:17
  47.5 4.6 %collective-permute-start.3 = (f32[2,256,10,1]{1,0,3,2:T(2,128)S(1)}, f32[2,256,10,1]{1,0,3,2:T(2,128)S(1)}, u32[]{:S(2)}, u32[]{:S(2)}) collective-permute-start(f32[2,256,10,1]{1,0,3,2:T(2,128)S(1)} %get-tuple-element.41), channel_id=1, source_target_pairs={{2,0},{4,2},{6,4},{8,6},{10,8},{12,10},{14,12},{16,14},{18,16},{20... | collective-permute-start | bytes 61448 | tf_op jit(solution)/shard_map/ppermute | solution.py:17
  52.1 2.9 copy.67
  55.0 9.7 %pad_maximum_fusion.2 = f32[2,256,10,258]{1,0,3,2:T(2,128)} fusion(f32[2,256,10,1]{1,0,3,2:T(2,128)S(1)} %collective-permute-done.3, f32[2,256,1,256]{1,0,3,2:T(2,128)S(1)} %collective-permute-done.1, f32[1,256,8,256]{1,0,3,2:T(1,128)} %copy-done, f32[1,256,8,256]{1,0,3,2:T(1,128)S(1)} %copy.43, f32[2,256,1,256]{1,0,3,2:T(2,128)S(1)} %collective-permute-done, ...), kind=kLoop, calls=%fused_computation.8 | loop fusion | flops 6604800 | bytes 10567680 | tf_op jit(solution)/shard_map/concatenate | solution.py:18
  64.8 10.4 %fusion.63 = (f32[1,256,10,258]{1,0,3,2:T(1,128)S(1)}, f32[1,256,10,258]{1,0,3,2:T(1,128)}) fusion(f32[2,256,10,258]{1,0,3,2:T(2,128)} %pad_maximum_fusion.2), kind=kLoop, calls=%fused_computation.141 | loop fusion | bytes 10567680 | tf_op jit(solution)/shard_map/slice | solution.py:33
  75.1 2.4 copy_bitcast_fusion
  77.6 0.6 fusion.27
  78.3 1.5 collective-permute-start.4
  79.7 1.3 collective-permute-start.5
  81.1 2.5 collective-permute-done.4
  83.6 4.4 %collective-permute-done.5 = f32[1,256,1,256]{1,3,2,0:T(8,128)S(1)} collective-permute-done((f32[1,256,1,256]{1,3,2,0:T(8,128)S(1)}, f32[1,256,1,256]{1,3,2,0:T(8,128)S(1)}, u32[]{:S(2)}, u32[]{:S(2)}) %collective-permute-start.5) | collective-permute-done | bytes 262176 | tf_op jit(solution)/shard_map/ppermute | solution.py:17
  88.3 1.5 copy-done.6
  89.8 4.6 %collective-permute-start.7 = (f32[1,256,10,1]{1,3,2,0:T(1,128)S(1)}, f32[1,256,10,1]{1,3,2,0:T(1,128)S(1)}, u32[]{:S(2)}, u32[]{:S(2)}) collective-permute-start(f32[1,256,10,1]{1,3,2,0:T(1,128)S(1)} %get-tuple-element.49), channel_id=1, source_target_pairs={{2,0},{4,2},{6,4},{8,6},{10,8},{12,10},{14,12},{16,14},{18,16},{20... | collective-permute-start | bytes 30728 | tf_op jit(solution)/shard_map/ppermute | solution.py:17
  94.5 3.2 copy.63
  98.3 2.7 copy.47
  101.0 2.4 pad_maximum_fusion.4
  103.8 1.3 copy-done.5
  105.7 2.8 multiply_bitcast_fusion.1
  108.6 1.5 collective-permute-start.8
  110.1 1.3 collective-permute-start.9
  113.1 5.7 %collective-permute-done.8 = f32[2,256,1,256]{1,3,2,0:T(8,128)S(1)} collective-permute-done((f32[2,256,1,256]{1,3,2,0:T(8,128)S(1)}, f32[2,256,1,256]{1,3,2,0:T(8,128)S(1)}, u32[]{:S(2)}, u32[]{:S(2)}) %collective-permute-start.8) | collective-permute-done | bytes 524320 | tf_op jit(solution)/shard_map/ppermute | solution.py:16
  118.8 4.1 %collective-permute-done.9 = f32[2,256,1,256]{1,3,2,0:T(8,128)S(1)} collective-permute-done((f32[2,256,1,256]{1,3,2,0:T(8,128)S(1)}, f32[2,256,1,256]{1,3,2,0:T(8,128)S(1)}, u32[]{:S(2)}, u32[]{:S(2)}) %collective-permute-start.9) | collective-permute-done | bytes 524320 | tf_op jit(solution)/shard_map/ppermute | solution.py:17
  123.1 4.5 %collective-permute-start.11 = (f32[2,256,10,1]{1,0,3,2:T(2,128)S(1)}, f32[2,256,10,1]{1,0,3,2:T(2,128)S(1)}, u32[]{:S(2)}, u32[]{:S(2)}) collective-permute-start(f32[2,256,10,1]{1,0,3,2:T(2,128)S(1)} %copy.50), channel_id=1, source_target_pairs={{2,0},{4,2},{6,4},{8,6},{10,8},{12,10},{14,12},{16,14},{18,16},{20... | collective-permute-start | bytes 61448 | tf_op jit(solution)/shard_map/ppermute | solution.py:17
  128.0 0.9 collective-permute-done.10
  129.0 2.1 pad_maximum_fusion.1
  131.7 1.1 copy-done.3
  132.8 0.6 fusion.17
  133.5 1.1 gather_fusion
  135.0 1.3 fusion.68
  136.4 0.8 fusion.66
  137.2 1.6 collective-permute-start.12
  138.8 1.3 collective-permute-start.13
  140.3 40.0 %psum.15 = f32[256]{0:T(256)S(1)} all-reduce(f32[256]{0:T(256)S(1)} %bitcast.156), channel_id=1, replica_groups=mesh['lon'=16,'lat'=2] {'lon','lat'}, use_global_device_ids=true, to_apply=%region_7.8 | all-reduce | flops 256 | bytes 2048 | tf_op jit(solution)/shard_map/psum | solution.py:69
  180.4 81.5 %all-reduce.3.cloned.1.call-done = f32[256,256]{0,1:T(8,128)} async-done(((f32[256,256]{0,1:T(8,128)}), f32[256,256]{0,1:T(8,128)}) %all-reduce.3.cloned.1.call-update) | async-done | bytes 262160 | tf_op jit(solution)/shard_map/psum | solution.py:69
  261.8 1.0 convert_add_fusion
  263.0 1.0 fusion.38
  264.0 11.7 %cholesky.49 = f32[128,128]{1,0:T(8,128)S(1)} custom-call(f32[128,128]{1,0:T(8,128)S(1)} %cholesky.115), custom_call_target="Cholesky" | custom-call | tf_op jit(solution)/shard_map/jit(cholesky)/cholesky | solution.py:71
  275.7 9.8 %custom-call.21 = f32[1,128,128]{1,2,0:T(8,128)S(1)} custom-call(f32[1,128,128]{2,1,0:T(8,128)S(1)} %get-tuple-element.57), custom_call_target="InvertDiagBlocksLowerTriangular" | custom-call | tf_op jit(solution)/shard_map/jit(cholesky)/cholesky | solution.py:71
  286.0 11.7 %cholesky.103 = f32[128,128]{1,0:T(8,128)S(1)} custom-call(f32[128,128]{1,0:T(8,128)S(1)} %convolution_subtract_fusion.1), custom_call_target="Cholesky" | custom-call | tf_op jit(solution)/shard_map/jit(cholesky)/cholesky | solution.py:71
  297.8 0.7 compare_reduce_fusion
  298.5 0.7 compare_reduce_fusion.1
  300.6 5.1 %while.1 = (s32[]{:T(128)}, f32[256,256]{1,0:T(8,128)S(1)}, s32[2,2]{1,0:T(2,128)S(1)}, f32[2,128,128]{2,1,0:T(8,128)}, s32[]{:T(128)}) while((s32[]{:T(128)}, f32[256,256]{1,0:T(8,128)S(1)}, s32[2,2]{1,0:T(2,128)S(1)}, f32[2,128,128]{2,1,0:T(8,128)}, s32[]{:T(128)}) %tuple.43), condition=%wide.while_cond, body=%wide.while_body.sunk | while | flops 2 | bytes 132705 | solution.py:72
  301.2 2.0 bitcast_dynamic-update-slice_fusion.2
  303.8 1.9 bitcast_dynamic-update-slice_fusion.2
  305.7 20.6 %custom-call.22 = f32[2,128,128]{1,2,0:T(8,128)S(1)} custom-call(f32[2,128,128]{2,1,0:T(8,128)} %get-tuple-element.12), custom_call_target="InvertDiagBlocksLowerTriangular" | custom-call | tf_op jit(solution)/shard_map/jit(_solve_triangular)/triangular_solve | solution.py:72
  328.6 1.2 pad_maximum_fusion.7
  329.8 4.4 %collective-permute-start.15 = (f32[1,256,10,1]{1,3,2,0:T(1,128)S(1)}, f32[1,256,10,1]{1,3,2,0:T(1,128)S(1)}, u32[]{:S(2)}, u32[]{:S(2)}) collective-permute-start(f32[1,256,10,1]{1,3,2,0:T(1,128)S(1)} %get-tuple-element.47), channel_id=1, source_target_pairs={{2,0},{4,2},{6,4},{8,6},{10,8},{12,10},{14,12},{16,14},{18,16},{20... | collective-permute-start | bytes 30728 | tf_op jit(solution)/shard_map/ppermute | solution.py:17
  334.3 2.7 copy.54
  337.0 2.4 pad_maximum_fusion.5
  339.8 1.3 copy-done.9
  341.7 1.1 fusion.15
  342.8 0.9 fusion.2
  343.7 7.1 %add_bitcast_fusion = f32[3,256,8,256]{1,3,2,0:T(8,128)} fusion(f32[3,8,256]{2,1,0:T(8,128)S(1)} %broadcast_multiply_fusion.2, f32[1,256,8,256]{1,3,2,0:T(8,128)S(1)} %get-tuple-element.30, f32[1,256,8,256]{1,3,2,0:T(8,128)S(1)} %get-tuple-element.29, f32[1,256,8,256]{1,3,2,0:T(8,128)S(1)} %bitcast.145, f32[128,256]{1,0:T(8,128)S(1)} %fusion.48, ...), kind=kOutput, calls=%fused_computation.4 | convolution fusion | flops 4838260736 | bytes 12870656 | tf_op jit(solution)/shard_map/nm,cnab->cmab/dot_general | solution.py:77
  350.8 6.6 %copy.59 = f32[3,256,8,256]{3,2,1,0:T(8,128)} copy(f32[3,256,8,256]{1,3,2,0:T(8,128)} %add_bitcast_fusion) | data formatting | bytes 12582912 | tf_op jit(solution)/shard_map/add | solution.py:78
  (108 shorter events, 10.6 us)
Async XLA Ops:
  6.5 255.3 %all-reduce.3.cloned.1.call-start = ((), (), s32[]{:S(2)}) async-start(), calls=%async_computation | async-start | bytes 524288 | tf_op jit(solution)/shard_map/psum | solution.py:69
  12.2 3.3 copy-start.12
  14.2 1.3 copy-start.4
  26.3 21.2 %copy-start = (f32[1,256,8,256]{1,0,3,2:T(1,128)}, f32[1,256,8,256]{1,0,3,2:T(1,128)S(1)}, u32[]{:S(2)}) copy-start(f32[1,256,8,256]{1,0,3,2:T(1,128)S(1)} %broadcast_multiply_fusion) | copy-start | bytes 6291460
  27.2 16.0 %collective-permute-start = (f32[2,256,1,256]{1,0,3,2:T(2,128)S(1)}, f32[2,256,1,256]{1,0,3,2:T(2,128)S(1)}, u32[]{:S(2)}, u32[]{:S(2)}) collective-permute-start(f32[2,256,1,256]{1,0,3,2:T(2,128)S(1)} %get-tuple-element.44), channel_id=1, source_target_pairs={{0,1},{2,3},{4,5},{6,7},{8,9},{10,11},{12,13},{14,15},{16,17},{18,... | collective-permute-start | bytes 1572872 | tf_op jit(solution)/shard_map/ppermute | solution.py:16
  32.1 15.3 %collective-permute-start.1 = (f32[2,256,1,256]{1,0,3,2:T(2,128)S(1)}, f32[2,256,1,256]{1,0,3,2:T(2,128)S(1)}, u32[]{:S(2)}, u32[]{:S(2)}) collective-permute-start(f32[2,256,1,256]{1,0,3,2:T(2,128)S(1)} %get-tuple-element.45), channel_id=1, source_target_pairs={{1,0},{3,2},{5,4},{7,6},{9,8},{11,10},{13,12},{15,14},{17,16},{19,... | collective-permute-start | bytes 1572872 | tf_op jit(solution)/shard_map/ppermute | solution.py:17
  47.5 7.6 %collective-permute-start.2 = (f32[2,256,10,1]{1,0,3,2:T(2,128)S(1)}, f32[2,256,10,1]{1,0,3,2:T(2,128)S(1)}, u32[]{:S(2)}, u32[]{:S(2)}) collective-permute-start(f32[2,256,10,1]{1,0,3,2:T(2,128)S(1)} %get-tuple-element.40), channel_id=1, source_target_pairs={{0,2},{2,4},{4,6},{6,8},{8,10},{10,12},{12,14},{14,16},{16,18},{18... | collective-permute-start | bytes 61448 | tf_op jit(solution)/shard_map/ppermute | solution.py:16
  47.5 7.5 %collective-permute-start.3 = (f32[2,256,10,1]{1,0,3,2:T(2,128)S(1)}, f32[2,256,10,1]{1,0,3,2:T(2,128)S(1)}, u32[]{:S(2)}, u32[]{:S(2)}) collective-permute-start(f32[2,256,10,1]{1,0,3,2:T(2,128)S(1)} %get-tuple-element.41), channel_id=1, source_target_pairs={{2,0},{4,2},{6,4},{8,6},{10,8},{12,10},{14,12},{16,14},{18,16},{20... | collective-permute-start | bytes 61448 | tf_op jit(solution)/shard_map/ppermute | solution.py:17
  75.1 2.4 copy-start.8
  77.5 3.5 copy-start.16
  78.2 10.1 %copy-start.2 = (f32[256,8,256]{0,2,1:T(8,128)}, f32[256,8,256]{0,2,1:T(8,128)S(1)}, u32[]{:S(2)}) copy-start(f32[256,8,256]{0,2,1:T(8,128)S(1)} %fusion.27) | copy-start | bytes 6291460
  78.3 5.3 %collective-permute-start.4 = (f32[1,256,1,256]{1,3,2,0:T(8,128)S(1)}, f32[1,256,1,256]{1,3,2,0:T(8,128)S(1)}, u32[]{:S(2)}, u32[]{:S(2)}) collective-permute-start(f32[1,256,1,256]{1,3,2,0:T(8,128)S(1)} %get-tuple-element.52), channel_id=1, source_target_pairs={{0,1},{2,3},{4,5},{6,7},{8,9},{10,11},{12,13},{14,15},{16,17},{18,... | collective-permute-start | bytes 786440 | tf_op jit(solution)/shard_map/ppermute | solution.py:16
  79.7 8.3 %collective-permute-start.5 = (f32[1,256,1,256]{1,3,2,0:T(8,128)S(1)}, f32[1,256,1,256]{1,3,2,0:T(8,128)S(1)}, u32[]{:S(2)}, u32[]{:S(2)}) collective-permute-start(f32[1,256,1,256]{1,3,2,0:T(8,128)S(1)} %get-tuple-element.53), channel_id=1, source_target_pairs={{1,0},{3,2},{5,4},{7,6},{9,8},{11,10},{13,12},{15,14},{17,16},{19,... | collective-permute-start | bytes 786440 | tf_op jit(solution)/shard_map/ppermute | solution.py:17
  88.3 1.5 copy-start.6
  89.8 11.2 %collective-permute-start.6 = (f32[1,256,10,1]{1,3,2,0:T(1,128)S(1)}, f32[1,256,10,1]{1,3,2,0:T(1,128)S(1)}, u32[]{:S(2)}, u32[]{:S(2)}) collective-permute-start(f32[1,256,10,1]{1,3,2,0:T(1,128)S(1)} %get-tuple-element.48), channel_id=1, source_target_pairs={{0,2},{2,4},{4,6},{6,8},{8,10},{10,12},{12,14},{14,16},{16,18},{18... | collective-permute-start | bytes 30728 | tf_op jit(solution)/shard_map/ppermute | solution.py:16
  89.8 11.2 %collective-permute-start.7 = (f32[1,256,10,1]{1,3,2,0:T(1,128)S(1)}, f32[1,256,10,1]{1,3,2,0:T(1,128)S(1)}, u32[]{:S(2)}, u32[]{:S(2)}) collective-permute-start(f32[1,256,10,1]{1,3,2,0:T(1,128)S(1)} %get-tuple-element.49), channel_id=1, source_target_pairs={{2,0},{4,2},{6,4},{8,6},{10,8},{12,10},{14,12},{16,14},{18,16},{20... | collective-permute-start | bytes 30728 | tf_op jit(solution)/shard_map/ppermute | solution.py:17
  94.5 9.3 %copy-start.18 = (f32[8]{0:T(128)}, f32[8]{0:T(128)S(1)}, u32[]{:S(2)}) copy-start(f32[8]{0:T(128)S(1)} %multiply_sine_fusion) | copy-start | bytes 100
  94.5 3.8 %copy-start.7 = (f32[1,256,10,256]{1,3,2,0:T(8,128)S(1)}, f32[1,256,10,256]{1,3,2,0:T(8,128)}, u32[]{:S(2)}) copy-start(f32[1,256,10,256]{1,3,2,0:T(8,128)} %copy-done.6) | copy-start | bytes 7864324
  103.5 1.6 copy-start.5
  103.5 2.2 copy-start.11
  108.5 14.4 %copy-start.1 = (f32[1,256,8,256]{1,3,2,0:T(8,128)}, f32[1,256,8,256]{1,3,2,0:T(8,128)S(1)}, u32[]{:S(2)}) copy-start(f32[1,256,8,256]{1,3,2,0:T(8,128)S(1)} %get-tuple-element.27) | copy-start | bytes 6291460
  108.5 4.0 %copy-start.20 = (f32[1,1,256]{2,1,0:T(1,128)S(1)}, f32[1,1,256]{2,1,0:T(1,128)}, u32[]{:S(2)}) copy-start(f32[1,1,256]{2,1,0:T(1,128)} %param.11) | copy-start | bytes 3076
  108.6 10.2 %collective-permute-start.8 = (f32[2,256,1,256]{1,3,2,0:T(8,128)S(1)}, f32[2,256,1,256]{1,3,2,0:T(8,128)S(1)}, u32[]{:S(2)}, u32[]{:S(2)}) collective-permute-start(f32[2,256,1,256]{1,3,2,0:T(8,128)S(1)} %get-tuple-element.42), channel_id=1, source_target_pairs={{0,1},{2,3},{4,5},{6,7},{8,9},{10,11},{12,13},{14,15},{16,17},{18,... | collective-permute-start | bytes 1572872 | tf_op jit(solution)/shard_map/ppermute | solution.py:16
  110.1 12.8 %collective-permute-start.9 = (f32[2,256,1,256]{1,3,2,0:T(8,128)S(1)}, f32[2,256,1,256]{1,3,2,0:T(8,128)S(1)}, u32[]{:S(2)}, u32[]{:S(2)}) collective-permute-start(f32[2,256,1,256]{1,3,2,0:T(8,128)S(1)} %get-tuple-element.43), channel_id=1, source_target_pairs={{1,0},{3,2},{5,4},{7,6},{9,8},{11,10},{13,12},{15,14},{17,16},{19,... | collective-permute-start | bytes 1572872 | tf_op jit(solution)/shard_map/ppermute | solution.py:17
  123.0 6.0 %collective-permute-start.10 = (f32[2,256,10,1]{1,0,3,2:T(2,128)S(1)}, f32[2,256,10,1]{1,0,3,2:T(2,128)S(1)}, u32[]{:S(2)}, u32[]{:S(2)}) collective-permute-start(f32[2,256,10,1]{1,0,3,2:T(2,128)S(1)} %copy.49), channel_id=1, source_target_pairs={{0,2},{2,4},{4,6},{6,8},{8,10},{10,12},{12,14},{14,16},{16,18},{18... | collective-permute-start | bytes 61448 | tf_op jit(solution)/shard_map/ppermute | solution.py:16
  123.1 6.0 %collective-permute-start.11 = (f32[2,256,10,1]{1,0,3,2:T(2,128)S(1)}, f32[2,256,10,1]{1,0,3,2:T(2,128)S(1)}, u32[]{:S(2)}, u32[]{:S(2)}) collective-permute-start(f32[2,256,10,1]{1,0,3,2:T(2,128)S(1)} %copy.50), channel_id=1, source_target_pairs={{2,0},{4,2},{6,4},{8,6},{10,8},{12,10},{14,12},{16,14},{18,16},{20... | collective-permute-start | bytes 61448 | tf_op jit(solution)/shard_map/ppermute | solution.py:17
  131.2 1.6 copy-start.3
  133.4 1.2 copy-start.13
  133.4 1.3 copy-start.17
  133.5 1.3 copy-start.21
  133.5 1.4 copy-start.14
  133.5 1.4 copy-start.15
  137.2 163.3 %copy-start.22 = (s32[2]{0:T(128)S(1)}, s32[2]{0:T(128)}, u32[]{:S(2)}) copy-start(s32[2]{0:T(128)} %iota_multiply_fusion) | copy-start | bytes 28
  137.2 191.3 %collective-permute-start.12 = (f32[1,256,1,256]{1,3,2,0:T(8,128)}, f32[1,256,1,256]{1,3,2,0:T(8,128)S(1)}, u32[]{:S(2)}, u32[]{:S(2)}) collective-permute-start(f32[1,256,1,256]{1,3,2,0:T(8,128)} %get-tuple-element.50), channel_id=1, source_target_pairs={{0,1},{2,3},{4,5},{6,7},{8,9},{10,11},{12,13},{14,15},{16,17},{18,... | collective-permute-start | bytes 786440 | tf_op jit(solution)/shard_map/ppermute | solution.py:16
  138.8 189.8 %collective-permute-start.13 = (f32[1,256,1,256]{1,3,2,0:T(8,128)}, f32[1,256,1,256]{1,3,2,0:T(8,128)}, u32[]{:S(2)}, u32[]{:S(2)}) collective-permute-start(f32[1,256,1,256]{1,3,2,0:T(8,128)} %get-tuple-element.51), channel_id=1, source_target_pairs={{1,0},{3,2},{5,4},{7,6},{9,8},{11,10},{13,12},{15,14},{17,16},{19,... | collective-permute-start | bytes 786440 | tf_op jit(solution)/shard_map/ppermute | solution.py:17
  329.8 7.2 %collective-permute-start.14 = (f32[1,256,10,1]{1,3,2,0:T(1,128)S(1)}, f32[1,256,10,1]{1,3,2,0:T(1,128)S(1)}, u32[]{:S(2)}, u32[]{:S(2)}) collective-permute-start(f32[1,256,10,1]{1,3,2,0:T(1,128)S(1)} %get-tuple-element.46), channel_id=1, source_target_pairs={{0,2},{2,4},{4,6},{6,8},{8,10},{10,12},{12,14},{14,16},{16,18},{18... | collective-permute-start | bytes 30728 | tf_op jit(solution)/shard_map/ppermute | solution.py:16
  329.8 7.2 %collective-permute-start.15 = (f32[1,256,10,1]{1,3,2,0:T(1,128)S(1)}, f32[1,256,10,1]{1,3,2,0:T(1,128)S(1)}, u32[]{:S(2)}, u32[]{:S(2)}) collective-permute-start(f32[1,256,10,1]{1,3,2,0:T(1,128)S(1)} %get-tuple-element.47), channel_id=1, source_target_pairs={{2,0},{4,2},{6,4},{8,6},{10,8},{12,10},{14,12},{16,14},{18,16},{20... | collective-permute-start | bytes 30728 | tf_op jit(solution)/shard_map/ppermute | solution.py:17
  339.5 1.6 copy-start.9
  339.5 2.2 copy-start.10
  339.5 2.2 copy-start.19
Sparse Core Ops, SparseCore 0:
  136.5 125.3 all-reduce.2
where the time goes:
time: 370 us; the launch traced here: 364 us
  waiting for transfers between devices  113 us (31%)
  other arithmetic  89.8 us (24%)
  local copies, waits for them, and re-layouts  61.1 us (17%)
  blocking collectives  40 us (11%)
  starting transfers between devices  32.9 us (9%)
  between operations  16.3 us (4%)
  matrix products  11.2 us (3%)
    psum x1, waiting for transfers between devices, shards(): gram, proj = lax.psum((gram, proj), ('lon', 'lat'))  81.5 us
    psum x1, blocking collectives, shards(): gram, proj = lax.psum((gram, proj), ('lon', 'lat'))  40 us
    another operation x7, other arithmetic, shards(): lower = jnp.linalg.cholesky(gram + eye)  34.7 us
    ppermute x8, starting transfers between devices, with_halo(): after = lax.ppermute(first, axis, down)  23.3 us
    another operation x3, other arithmetic, shards(): inv_lower = jax.scipy.linalg.solve_triangular(lower, eye, lower=True)  21.2 us
    unnamed x52, local copies, waits for them, and re-layouts  20.5 us
    ppermute x8, waiting for transfers between devices, with_halo(): before = lax.ppermute(last, axis, up)  18.9 us
    concatenate x6, other arithmetic, with_halo(): value = jnp.concatenate([before, value, after], axis=dim)  18.2 us
  transfers between devices with their start and end apart: 17, of which 9 were waited for; matrix products, arithmetic and copies ran while one was open for 22% of the time, Pallas kernels for 0%

commit v1 on v0

v1 whole, which is shorter than its diff:
```python
import functools
import math

import jax
import jax.numpy as jnp
from jax import lax
from jax.experimental import pallas as pl
from jax.experimental.pallas import tpu as pltpu
from jax.sharding import PartitionSpec as P

MESH = pl.DeviceIdType.MESH
PAD = 8


def forecast_kernel(nlon, nlat, members, rows, cols, state, bath, index, count, value, sd, fh, fu, fv,
                    pay, raw, hp, fxp, fy, brep, rbuf, csend, crecv, hx, lsem, rs, rr, cs, cr):
    lon, lat = lax.axis_index("lon"), lax.axis_index("lat")
    west, east = lax.rem(lon + nlon - 1, nlon), lax.rem(lon + 1, nlon)
    last = rows - 1
    has_n, has_s = lat > 0, lat < nlat - 1

    tiles = cols // 128
    loads = [[pltpu.make_async_copy(state.at[c, :, pl.ds(128 * i, 128)], raw.at[c, i], lsem.at[c, i])
              for i in range(tiles)] for c in range(3)]
    for c in (2, 1, 0):
        for load in loads[c]:
            load.start()
    barrier = pltpu.get_barrier_semaphore()
    for side in (west, east):
        pl.semaphore_signal(barrier, inc=1, device_id={"lon": side}, device_id_type=MESH)

    @pl.when(has_n)
    def _():
        pl.semaphore_signal(barrier, inc=1, device_id={"lat": lat - 1}, device_id_type=MESH)

    @pl.when(has_s)
    def _():
        pl.semaphore_signal(barrier, inc=1, device_id={"lat": lat + 1}, device_id_type=MESH)

    bt = bath[...].T
    for r in range(rows):
        brep[r] = jnp.broadcast_to(bt[:, r:r + 1], (cols, 128))
    zero = jnp.zeros((cols, members), jnp.float32)

    @pl.when(jnp.logical_not(has_n))
    def _():
        for e in range(4):
            rbuf[e, 0] = zero

    @pl.when(jnp.logical_not(has_s))
    def _():
        for e in range(4):
            rbuf[e, 1] = zero

    pl.semaphore_wait(barrier, 2 + jnp.minimum(lat, 1) + jnp.minimum(nlat - 1 - lat, 1))

    def row_copy(e, north):
        if e % 2 == 0:
            src = fy.at[0 if north else last]
        else:
            src = hp.at[0 if north else last, pl.ds(PAD, cols)]
        return pltpu.make_async_remote_copy(
            src_ref=src, dst_ref=rbuf.at[e, 1 if north else 0],
            send_sem=rs.at[e, 0 if north else 1], recv_sem=rr.at[e, 1 if north else 0],
            device_id={"lat": lat - 1 if north else lat + 1}, device_id_type=MESH)

    def row_recv(e, side):
        return pltpu.make_async_remote_copy(
            src_ref=rbuf.at[e, side], dst_ref=rbuf.at[e, side], send_sem=rs.at[e, side],
            recv_sem=rr.at[e, side], device_id={"lat": lat - 1 if side == 0 else lat + 1},
            device_id_type=MESH)

    def send_rows(e):
        @pl.when(has_n)
        def _():
            row_copy(e, True).start()

        @pl.when(has_s)
        def _():
            row_copy(e, False).start()

    def wait_rows(e):
        @pl.when(has_n)
        def _():
            row_copy(e, True).wait_send()
            row_recv(e, 0).wait_recv()

        @pl.when(has_s)
        def _():
            row_copy(e, False).wait_send()
            row_recv(e, 1).wait_recv()

    def col_copy(e, side):
        return pltpu.make_async_remote_copy(
            src_ref=csend.at[e, side], dst_ref=crecv.at[e, 1 - side],
            send_sem=cs.at[e, side], recv_sem=cr.at[e, 1 - side],
            device_id={"lon": west if side == 0 else east}, device_id_type=MESH)

    def send_cols(e, ref):
        for r in range(rows):
            csend[e, 0, r:r + 1, :] = ref[r, PAD:PAD + 1, :]
            csend[e, 1, r:r + 1, :] = ref[r, PAD + cols - 1:PAD + cols, :]
        col_copy(e, 0).start()
        col_copy(e, 1).start()

    def wait_cols(e, ref):
        for side in (0, 1):
            col_copy(e, side).wait()
        for r in range(rows):
            ref[r, PAD - 1:PAD, :] = crecv[e, 0, r:r + 1, :]
            ref[r, PAD + cols:PAD + cols + 1, :] = crecv[e, 1, r:r + 1, :]

    def slab(c, r):
        return jnp.concatenate(
            [raw[c, i, pl.ds(r, members, stride=rows), :].T for i in range(tiles)], axis=0)

    def bmul(r, x):
        b = brep[r]
        return jnp.concatenate([x[:, i:i + 128] * b for i in range(0, members, 128)], axis=1)

    def dcol(ref, r):
        return ref[r, PAD + 1:PAD + cols + 1, :] - ref[r, PAD - 1:PAD + cols - 1, :]

    def fcor(r):
        row = (lat * rows + r).astype(jnp.float32)
        angle = jnp.full((1, members), (row + 0.5) / (rows * nlat) - 0.5, jnp.float32)
        return jnp.sin(math.pi / 3.0 * angle)

    for load in loads[2]:
        load.wait()
    for r in (0, last):
        v = slab(2, r)
        fv[r] = v
        fy[r] = bmul(r, v)
    send_rows(0)
    for load in loads[1]:
        load.wait()
    for r in range(rows):
        u = slab(1, r)
        fu[r] = u
        fxp[r, PAD:PAD + cols, :] = bmul(r, u)
    send_cols(0, fxp)
    for r in range(1, last):
        v = slab(2, r)
        fv[r] = v
        fy[r] = bmul(r, v)
    for load in loads[0]:
        load.wait()
    for r in range(rows):
        hp[r, PAD:PAD + cols, :] = slab(0, r)

    def height(r, up, down):
        div = dcol(fxp, r) + down - up
        hp[r, PAD:PAD + cols, :] = hp[r, PAD:PAD + cols, :] - 0.25 * div

    def wind(r, up, down, flux):
        f = fcor(r)
        u, v = fu[r], fv[r]
        un = u + 0.5 * (f * v - 0.5 * dcol(hp, r))
        vn = v - 0.5 * (f * u + 0.5 * (down - up))
        fu[r] = un
        fv[r] = vn
        if flux:
            fxp[r, PAD:PAD + cols, :] = bmul(r, un)
            fy[r] = bmul(r, vn)

    def hrow(r):
        return hp[r, PAD:PAD + cols, :]

    for step in range(2):
        e = 2 * step
        wait_cols(e, fxp)
        if step == 1:
            @pl.loop(1, last)
            def _(r):
                height(r, fy[r - 1], fy[r + 1])
        wait_rows(e)
        height(0, rbuf[e, 0], fy[1])
        height(last, fy[last - 1], rbuf[e, 1])
        send_rows(e + 1)
        if step == 0:
            @pl.loop(1, last)
            def _(r):
                height(r, fy[r - 1], fy[r + 1])
        send_cols(e + 1, hp)
        if step == 1:
            slots = hx.shape[0]

            @pl.loop(0, slots // 8)
            def _(t):
                parts = []
                for k in range(8):
                    cell = index[0, t * 8 + k]
                    parts.append(hp[cell // cols, pl.ds(PAD + lax.rem(cell, cols), 1), :])
                hx[pl.ds(t * 8, 8), :] = jnp.concatenate(parts, axis=0)

            x = hx[...]
            info = jnp.concatenate([value[...], sd[...], jnp.zeros((6, slots), jnp.float32)], axis=0).T
            sigma = info[:, 1:2] * (math.sqrt(slots * nlon * nlat) / 16.0)
            valid = (lax.broadcasted_iota(jnp.int32, (slots, 1), 0) < count[0, 0]).astype(jnp.float32)
            mean = jnp.sum(x, axis=1, keepdims=True) * (1.0 / members)
            yp = (x - mean) * (valid / (math.sqrt(members - 1) * sigma))
            innov = (info[:, 0:1] - mean) * (valid / sigma)
            proj = jnp.sum(yp * innov, axis=0, keepdims=True)
            pay[...] = jnp.dot(yp.T, yp, precision=lax.Precision.HIGHEST,
                               preferred_element_type=jnp.float32)
            half = members // 2
            pay[members - 2:members - 1, 0:half] = proj[:, :half]
            pay[members - 1:members, 0:half] = proj[:, half:]
        wait_cols(e + 1, hp)

        @pl.loop(1, last)
        def _(r):
            wind(r, hrow(r - 1), hrow(r + 1), step == 0)
        wait_rows(e + 1)
        wind(0, rbuf[e + 1, 0], hrow(1), step == 0)
        wind(last, hrow(last - 1), rbuf[e + 1, 1], step == 0)
        if step == 0:
            send_rows(2)
            send_cols(2, fxp)

    for r in range(rows):
        fh[r] = hrow(r)


def forecast(nlon, nlat, state, bathymetry, obs_index, obs_count, obs_value, obs_sd):
    _, members, rows, cols = state.shape
    slots = obs_index.shape[2]
    f32 = jnp.float32
    field = jax.ShapeDtypeStruct((rows, cols, members), f32)
    vmem, smem = pl.BlockSpec(memory_space=pltpu.VMEM), pl.BlockSpec(memory_space=pltpu.SMEM)
    return pl.pallas_call(
        functools.partial(forecast_kernel, nlon, nlat, members, rows, cols),
        out_shape=[field, field, field, jax.ShapeDtypeStruct((members, members), f32)],
        in_specs=[pl.BlockSpec(memory_space=pl.ANY), vmem, smem, smem, vmem, vmem],
        out_specs=[vmem] * 4,
        scratch_shapes=[
            pltpu.VMEM((3, cols // 128, members * rows, 128), f32),
            pltpu.VMEM((rows, cols + 2 * PAD, members), f32),
            pltpu.VMEM((rows, cols + 2 * PAD, members), f32),
            pltpu.VMEM((rows, cols, members), f32),
            pltpu.VMEM((rows, cols, 128), f32),
            pltpu.VMEM((4, 2, cols, members), f32),
            pltpu.VMEM((4, 2, rows, members), f32),
            pltpu.VMEM((4, 2, rows, members), f32),
            pltpu.VMEM((slots, members), f32),
            pltpu.SemaphoreType.DMA((3, cols // 128)),
            pltpu.SemaphoreType.DMA((4, 2)),
            pltpu.SemaphoreType.DMA((4, 2)),
            pltpu.SemaphoreType.DMA((4, 2)),
            pltpu.SemaphoreType.DMA((4, 2)),
        ],
        compiler_params=pltpu.CompilerParams(
            collective_id=0, has_side_effects=True, vmem_limit_bytes=52 * 2**20),
    )(state.reshape(3, members * rows, cols), bathymetry, obs_index.reshape(1, slots), obs_count,
      obs_value.reshape(1, slots), obs_sd.reshape(1, slots))


def sum_kernel(nlon, nlat, size, part, out, other, acc, parts, whole, back, ps, pr, ss, sr, gs, gr, qs, qr):
    lon, lat = lax.axis_index("lon"), lax.axis_index("lat")
    core, pair = lax.rem(lon, 2), lon // 2
    npair = nlon // 2
    peers = npair * nlat
    half = size // 2
    owners = min(peers, half // 8)
    chunk = half // owners
    me = lat * npair + pair
    partner = {"lon": lon + 1 - 2 * core}

    def device(p):
        return {"lon": 2 * lax.rem(p, npair) + core, "lat": p // npair}

    barrier = pltpu.get_barrier_semaphore()
    pl.semaphore_signal(barrier, inc=1, device_id=partner, device_id_type=MESH)

    @pl.loop(1, peers)
    def _(d):
        pl.semaphore_signal(barrier, inc=1, device_id=device(lax.rem(me + d, peers)), device_id_type=MESH)

    pl.semaphore_wait(barrier, peers)
    mine = pl.ds(pl.multiple_of(core * half, half), half)
    theirs = pl.ds(pl.multiple_of((1 - core) * half, half), half)

    def guard(cond, run):
        if owners == peers:
            run()
        else:
            pl.when(cond)(run)

    first = pltpu.make_async_remote_copy(
        src_ref=part.at[theirs], dst_ref=other, send_sem=ps, recv_sem=pr,
        device_id=partner, device_id_type=MESH)
    first.start()
    first.wait()
    acc[...] = part[mine, :] + other[...]

    def scatter(p, frm):
        return pltpu.make_async_remote_copy(
            src_ref=acc.at[pl.ds(pl.multiple_of(p * chunk, chunk), chunk)], dst_ref=parts.at[frm],
            send_sem=ss.at[p], recv_sem=sr.at[frm], device_id=device(p), device_id_type=MESH)

    def arrive(frm):
        return pltpu.make_async_remote_copy(
            src_ref=parts.at[frm], dst_ref=parts.at[frm],
            send_sem=ss.at[0], recv_sem=sr.at[frm], device_id=device(frm), device_id_type=MESH)

    @pl.loop(1, peers)
    def _(d):
        p = lax.rem(me + d, peers)
        guard(p < owners, lambda: scatter(p, me).start())

    def collect():
        total = acc[pl.ds(pl.multiple_of(me * chunk, chunk), chunk), :]

        def body(d, total):
            frm = lax.rem(me + d, peers)
            arrive(frm).wait_recv()
            return total + parts[frm]
        whole[me] = lax.fori_loop(1, peers, body, total)

    guard(me < owners, collect)

    @pl.loop(1, peers)
    def _(d):
        p = lax.rem(me + d, peers)
        guard(p < owners, lambda: scatter(p, me).wait_send())

    def spread(p, frm):
        return pltpu.make_async_remote_copy(
            src_ref=whole.at[frm], dst_ref=whole.at[frm],
            send_sem=gs.at[p], recv_sem=gr.at[frm], device_id=device(p), device_id_type=MESH)

    def send_all():
        @pl.loop(1, peers)
        def _(d):
            p = lax.rem(me + d, peers)
            spread(p, me).start()

    guard(me < owners, send_all)

    @pl.loop(1, peers)
    def _(d):
        p = lax.rem(me + d, peers)
        guard(p < owners, lambda: spread(p, p).wait_recv())

    last = pltpu.make_async_remote_copy(
        src_ref=whole, dst_ref=back, send_sem=qs, recv_sem=qr,
        device_id=partner, device_id_type=MESH)
    last.start()

    def sent_all():
        @pl.loop(1, peers)
        def _(d):
            p = lax.rem(me + d, peers)
            spread(p, me).wait_send()

    guard(me < owners, sent_all)
    out[mine, :] = whole[...].reshape(half, size)
    last.wait()
    out[theirs, :] = back[...].reshape(half, size)


def total_sum(nlon, nlat, part):
    size = part.shape[0]
    half, peers = size // 2, nlon // 2 * nlat
    owners = min(peers, half // 8)
    chunk = half // owners
    f32 = jnp.float32
    dma = pltpu.SemaphoreType.DMA
    vmem = pl.BlockSpec(memory_space=pltpu.VMEM)
    return pl.pallas_call(
        functools.partial(sum_kernel, nlon, nlat, size),
        out_shape=jax.ShapeDtypeStruct((size, size), f32),
        in_specs=[vmem],
        out_specs=vmem,
        scratch_shapes=[
            pltpu.VMEM((half, size), f32), pltpu.VMEM((half, size), f32),
            pltpu.VMEM((peers, chunk, size), f32), pltpu.VMEM((owners, chunk, size), f32),
            pltpu.VMEM((owners, chunk, size), f32),
            dma, dma, dma((peers,)), dma((peers,)), dma((peers,)), dma((peers,)), dma, dma,
        ],
        compiler_params=pltpu.CompilerParams(
            collective_id=1, has_side_effects=True, vmem_limit_bytes=32 * 2**20),
    )(part)


def split(x):
    hi = x.astype(jnp.bfloat16)
    return hi, (x - hi.astype(jnp.float32)).astype(jnp.bfloat16)


def invert(gram, size):
    lane = lax.broadcasted_iota(jnp.int32, (8, size), 1)
    sub = lax.broadcasted_iota(jnp.int32, (8, size), 0)
    sub1 = lax.broadcasted_iota(jnp.int32, (8, 1), 0)
    blocks = [gram[8 * t:8 * t + 8, :] + (lane == sub + 8 * t).astype(jnp.float32)
              for t in range(size // 8)]
    done = []
    for t in range(size // 8):
        base = 8 * t
        row = blocks[t]
        diag = [row[:, base + q:base + q + 1] for q in range(8)]
        inv = jnp.zeros((8, 1), jnp.float32)
        rsq = jnp.zeros((8, 1), jnp.float32)
        for k in range(8):
            pivot = diag[k][k:k + 1, :]
            recip = 1.0 / pivot
            inv = jnp.where(sub1 == k, recip, inv)
            rsq = jnp.where(sub1 == k, lax.rsqrt(pivot), rsq)
            if k < 7:
                f = jnp.where(sub1 > k, diag[k] * recip, 0.0)
                for q in range(k + 1, 8):
                    diag[q] = diag[q] - f * diag[q][k:k + 1, :]
                row = jnp.where((lane == base + k) & (sub > k), -f, row - f * row[k:k + 1, :])
        inpanel = (lane >= base) & (lane < base + 8)
        low = jnp.where(lane == base + sub, 1.0, jnp.where(lane > base + sub, 0.0, row))
        done.append(low * rsq)
        if t + 1 < size // 8:
            used = jnp.where(inpanel, low, row)
            factor = (row * inv).T
            for s in range(t + 1, size // 8):
                fac = factor[8 * s:8 * s + 8, :]
                new = jnp.where(inpanel, 0.0, blocks[s])
                for k in range(8):
                    new = new - fac[:, k:k + 1] * used[k:k + 1, :]
                blocks[s] = new
    return jnp.concatenate(done, axis=0)


def mix_kernel(members, gram, fh, fu, fv, out, hi, lo):
    @pl.when((pl.program_id(0) == 0) & (pl.program_id(1) == 0))
    def _():
        g = gram[...]
        half = members // 2
        proj = jnp.concatenate([g[members - 2:members - 1, :half], g[members - 1:members, :half]], axis=1)
        inv = invert(gram, members)
        part = jnp.sum(inv * proj, axis=1, keepdims=True)
        weights = jnp.sum(inv * part, axis=0, keepdims=True)
        t = inv + weights * (1.0 / math.sqrt(members - 1))
        t = t + (1.0 - jnp.sum(t, axis=1, keepdims=True)) * (1.0 / members)
        a, b = split(t)
        hi[...] = a
        lo[...] = b

    def mix(ref):
        dims = (((1,), (1,)), ((), ()))
        dot = functools.partial(lax.dot_general, dimension_numbers=dims, preferred_element_type=jnp.float32)
        rows = ref.shape[0]
        for r in range(rows):
            a, b = split(ref[r])
            out[0, pl.ds(r, members, stride=rows), :] = (
                dot(hi[...], a) + dot(hi[...], b) + dot(lo[...], a))

    for c, ref in enumerate((fh, fu, fv)):
        pl.when(pl.program_id(0) == c)(functools.partial(mix, ref))


def mixing(gram, fields):
    rows, cols, members = fields[0].shape
    width = 128
    steps = cols // width

    def spec(c):
        return pl.BlockSpec((rows, width, members), lambda i, j: (0, jnp.where(i == c, j, jnp.where(i < c, 0, steps - 1)), 0))

    out = pl.pallas_call(
        functools.partial(mix_kernel, members),
        grid=(3, steps),
        out_shape=jax.ShapeDtypeStruct((3, members * rows, cols), jnp.float32),
        in_specs=[pl.BlockSpec((members, members), lambda i, j: (0, 0))] + [spec(c) for c in range(3)],
        out_specs=pl.BlockSpec((1, members * rows, width), lambda i, j: (i, 0, j)),
        scratch_shapes=[pltpu.VMEM((members, members), jnp.bfloat16)] * 2,
        compiler_params=pltpu.CompilerParams(vmem_limit_bytes=48 * 2**20),
    )(gram, *fields)
    return out.reshape(3, members, rows, cols)


def shards(nlon, nlat, state, bathymetry, obs_index, obs_count, obs_value, obs_sd):
    h, u, v, part = forecast(nlon, nlat, state, bathymetry, obs_index, obs_count, obs_value, obs_sd)
    gram = total_sum(nlon, nlat, part)
    return mixing(gram, (h, u, v))


def solution(mesh):
    return jax.shard_map(
        functools.partial(shards, mesh.shape["lon"], mesh.shape["lat"]),
        mesh=mesh,
        in_specs=(
            P(None, None, "lat", "lon"),
            P("lat", "lon"),
            P("lat", "lon", None),
            P("lat", "lon"),
            P("lat", "lon", None),
            P("lat", "lon", None),
        ),
        out_specs=P(None, None, "lat", "lon"),
        check_vma=False,
    )
```

time: 370 us -> 110 us (0.30); the launches traced: 364 us -> 110 us
  waiting for transfers between devices: 113 us -> 0 us
  Pallas kernels: 0 us -> 103 us
  other arithmetic: 89.8 us -> 0 us
  local copies, waits for them, and re-layouts: 61.1 us -> 5.9 us
  blocking collectives: 40 us -> 0 us
  starting transfers between devices: 32.9 us -> 0 us
  between operations: 16.3 us -> 0.69 us
  matrix products: 11.2 us -> 0 us
    pallas_call x0 -> x3, Pallas kernels: none -> 103 us  [the longest x1 49.7 us: mixing(): pl.pallas_call(functools.partial(mix_kernel, members), grid=(3, steps), o...]
    psum x1 -> x0, waiting for transfers between devices: 81.5 us -> none  [shards(): gram, proj = lax.psum((gram, proj), ('lon', 'lat'))]
    another operation x12 -> x0, other arithmetic: 59.8 us -> none  [the longest x7 34.7 us: shards(): lower = jnp.linalg.cholesky(gram + eye)]
    psum x1 -> x0, blocking collectives: 40 us -> none  [shards(): gram, proj = lax.psum((gram, proj), ('lon', 'lat'))]
    ppermute x16 -> x0, starting transfers between devices: 32.9 us -> none  [the longest x8 23.3 us: with_halo(): after = lax.ppermute(first, axis, down)]
    ppermute x16 -> x0, waiting for transfers between devices: 31.7 us -> none  [the longest x8 18.9 us: with_halo(): before = lax.ppermute(last, axis, up)]
    concatenate x6 -> x0, other arithmetic: 18.2 us -> none  [with_halo(): value = jnp.concatenate([before, value, after], axis=dim)]
    slice x8 -> x0, local copies, waits for them, and re-layouts: 17 us -> none  [the longest x1 10.4 us: new_height(): flux[0][:, 1:-1, 2:] - flux[0][:, 1:-1, :-2] + flux[1][:, 2:, 1:-1]]
  transfers between devices with their start and end apart: 17 -> 0, of which waited for: 9 -> 0; matrix products, arithmetic and copies ran while one was open for 22% -> 0% of each run, Pallas kernels for 0% -> 0%
where the time goes in v1:
time: 110 us
  Pallas kernels  103 us (94%)
  local copies, waits for them, and re-layouts  5.9 us (5%)
    pallas_call x1, Pallas kernels, mixing(): pl.pallas_call(functools.partial(mix_kernel, members), grid=(3, steps), o...  49.7 us
    pallas_call x1, Pallas kernels, forecast(): pl.pallas_call(functools.partial(forecast_kernel, nlon, nlat, members, ro...  34.5 us
    pallas_call x1, Pallas kernels, total_sum(): pl.pallas_call(functools.partial(sum_kernel, nlon, nlat, size), out_shape...  18.8 us
    unnamed x12, local copies, waits for them, and re-layouts  5.9 us

profile of v1, /device:TPU:0, one launch (start us, length us, event | category | flops | bytes accessed | tf_op | source)
XLA Modules:
  0.0 109.7 jit_solution(8592481341918852957)
XLA Ops:
  0.7 0.0 copy-start.2
  0.7 0.7 copy-done.2
  1.4 0.0 copy-start.3
  1.4 0.7 copy-done.3
  2.0 0.0 copy-start.4
  2.0 0.7 copy-done.4
  2.7 0.0 copy-start.5
  2.7 0.7 copy-done.5
  3.4 34.5 %shard_map.64 = (f32[8,256,256]{2,1,0:T(8,128)}, f32[8,256,256]{2,1,0:T(8,128)}, f32[8,256,256]{2,1,0:T(8,128)}, f32[256,256]{1,0:T(8,128)S(1)}) custom-call(f32[3,2048,256]{2,1,0:T(8,128)} %bitcast.8, f32[8,256]{1,0:T(8,128)S(1)} %copy-done.2, s32[1,256]{1,0:T(1,128)S(1)} %bitcast.5, s32[1,1]{1,0:T(1,128)S(6)} %copy.7.count, f32[1,256]{1,0:T(1,128)S(1)} %bitcast.6, ...), custom_call_target="tpu_custom_call" | custom-call | tf_op jit(solution)/shard_map/pallas_call | solution.py:232
  37.9 18.8 %shard_map.65.gram = f32[256,256]{1,0:T(8,128)S(1)} custom-call(f32[256,256]{1,0:T(8,128)S(1)} %get-tuple-element.9.part), custom_call_target="tpu_custom_call" | custom-call | tf_op jit(solution)/shard_map/pallas_call | solution.py:371
  56.7 0.0 copy-start
  56.8 1.6 %copy-done = f32[8,256,256]{2,1,0:T(8,128)S(1)} copy-done((f32[8,256,256]{2,1,0:T(8,128)S(1)}, f32[8,256,256]{2,1,0:T(8,128)}, u32[]{:S(2)}) %copy-start) | copy-done | bytes 2097176
  58.3 0.0 copy-start.1
  58.3 1.6 %copy-done.1 = f32[8,256,256]{2,1,0:T(8,128)S(1)} copy-done((f32[8,256,256]{2,1,0:T(8,128)S(1)}, f32[8,256,256]{2,1,0:T(8,128)}, u32[]{:S(2)}) %copy-start.1) | copy-done | bytes 2097176
  59.9 49.7 %shard_map.66 = f32[3,2048,256]{2,1,0:T(8,128)} custom-call(f32[256,256]{1,0:T(8,128)S(1)} %shard_map.65.gram, f32[8,256,256]{2,1,0:T(8,128)S(1)} %copy-done, f32[8,256,256]{2,1,0:T(8,128)S(1)} %copy-done.1, f32[8,256,256]{2,1,0:T(8,128)} %get-tuple-element.12.fv), custom_call_target="tpu_custom_call" | custom-call | tf_op jit(solution)/shard_map/pallas_call | solution.py:466
Async XLA Ops:
  0.7 0.7 copy-start.2
  1.4 0.7 copy-start.3
  2.0 0.7 copy-start.4
  2.7 0.7 copy-start.5
  56.7 1.6 %copy-start = (f32[8,256,256]{2,1,0:T(8,128)S(1)}, f32[8,256,256]{2,1,0:T(8,128)}, u32[]{:S(2)}) copy-start(f32[8,256,256]{2,1,0:T(8,128)} %get-tuple-element.10.fh) | copy-start | bytes 6291460
  58.3 1.6 %copy-start.1 = (f32[8,256,256]{2,1,0:T(8,128)S(1)}, f32[8,256,256]{2,1,0:T(8,128)}, u32[]{:S(2)}) copy-start(f32[8,256,256]{2,1,0:T(8,128)} %get-tuple-element.11.fu) | copy-start | bytes 6291460

commit v2 on v1

--- a/solution.py
+++ b/solution.py
@@ -12,8 +12,9 @@
 PAD = 8
 
 
-def forecast_kernel(nlon, nlat, members, rows, cols, state, bath, index, count, value, sd, fh, fu, fv,
-                    pay, raw, hp, fxp, fy, brep, rbuf, csend, crecv, hx, lsem, rs, rr, cs, cr):
+def forecast_kernel(nlon, nlat, members, rows, cols, state, bath_at, index_at, count_at, value_at, sd_at,
+                    out_h, out_u, out_v, pay, raw, hp, fu, fv, fxp, fy, brep, rbuf, csend, crecv, hx,
+                    bath, index, count, value, sd, lsem, isem, osem, rs, rr, cs, cr):
     lon, lat = lax.axis_index("lon"), lax.axis_index("lat")
     west, east = lax.rem(lon + nlon - 1, nlon), lax.rem(lon + 1, nlon)
     last = rows - 1
@@ -25,6 +26,10 @@
     for c in (2, 1, 0):
         for load in loads[c]:
             load.start()
+    small = [pltpu.make_async_copy(src, dst, isem.at[i]) for i, (src, dst) in enumerate((
+        (bath_at, bath), (index_at, index), (count_at, count), (value_at, value), (sd_at, sd)))]
+    for load in small:
+        load.start()
     barrier = pltpu.get_barrier_semaphore()
     for side in (west, east):
         pl.semaphore_signal(barrier, inc=1, device_id={"lon": side}, device_id_type=MESH)
@@ -37,6 +42,7 @@
     def _():
         pl.semaphore_signal(barrier, inc=1, device_id={"lat": lat + 1}, device_id_type=MESH)
 
+    small[0].wait()
     bt = bath[...].T
     for r in range(rows):
         brep[r] = jnp.broadcast_to(bt[:, r:r + 1], (cols, 128))
@@ -167,6 +173,11 @@
     def hrow(r):
         return hp[r, PAD:PAD + cols, :]
 
+    out_copies = [
+        pltpu.make_async_copy(hp.at[:, pl.ds(PAD, cols)], out_h, osem.at[0]),
+        pltpu.make_async_copy(fu, out_u, osem.at[1]),
+        pltpu.make_async_copy(fv, out_v, osem.at[2]),
+    ]
     for step in range(2):
         e = 2 * step
         wait_cols(e, fxp)
@@ -185,6 +196,9 @@
         send_cols(e + 1, hp)
         if step == 1:
             slots = hx.shape[0]
+            out_copies[0].start()
+            for load in small[1:]:
+                load.wait()
 
             @pl.loop(0, slots // 8)
             def _(t):
@@ -219,8 +233,10 @@
             send_rows(2)
             send_cols(2, fxp)
 
-    for r in range(rows):
-        fh[r] = hrow(r)
+    out_copies[1].start()
+    out_copies[2].start()
+    for copy in out_copies:
+        copy.wait()
 
 
 def forecast(nlon, nlat, state, bathymetry, obs_index, obs_count, obs_value, obs_sd):
@@ -228,15 +244,17 @@
     slots = obs_index.shape[2]
     f32 = jnp.float32
     field = jax.ShapeDtypeStruct((rows, cols, members), f32)
-    vmem, smem = pl.BlockSpec(memory_space=pltpu.VMEM), pl.BlockSpec(memory_space=pltpu.SMEM)
+    vmem, hbm = pl.BlockSpec(memory_space=pltpu.VMEM), pl.BlockSpec(memory_space=pl.ANY)
     return pl.pallas_call(
         functools.partial(forecast_kernel, nlon, nlat, members, rows, cols),
         out_shape=[field, field, field, jax.ShapeDtypeStruct((members, members), f32)],
-        in_specs=[pl.BlockSpec(memory_space=pl.ANY), vmem, smem, smem, vmem, vmem],
-        out_specs=[vmem] * 4,
+        in_specs=[hbm] * 6,
+        out_specs=[hbm] * 3 + [vmem],
         scratch_shapes=[
             pltpu.VMEM((3, cols // 128, members * rows, 128), f32),
             pltpu.VMEM((rows, cols + 2 * PAD, members), f32),
+            pltpu.VMEM((rows, cols, members), f32),
+            pltpu.VMEM((rows, cols, members), f32),
             pltpu.VMEM((rows, cols + 2 * PAD, members), f32),
             pltpu.VMEM((rows, cols, members), f32),
             pltpu.VMEM((rows, cols, 128), f32),
@@ -244,7 +262,14 @@
             pltpu.VMEM((4, 2, rows, members), f32),
             pltpu.VMEM((4, 2, rows, members), f32),
             pltpu.VMEM((slots, members), f32),
+            pltpu.VMEM((rows, cols), f32),
+            pltpu.SMEM((1, slots), jnp.int32),
+            pltpu.SMEM((1, 1), jnp.int32),
+            pltpu.VMEM((1, slots), f32),
+            pltpu.VMEM((1, slots), f32),
             pltpu.SemaphoreType.DMA((3, cols // 128)),
+            pltpu.SemaphoreType.DMA((5,)),
+            pltpu.SemaphoreType.DMA((3,)),
             pltpu.SemaphoreType.DMA((4, 2)),
             pltpu.SemaphoreType.DMA((4, 2)),
             pltpu.SemaphoreType.DMA((4, 2)),
@@ -380,7 +405,7 @@
             dma, dma, dma((peers,)), dma((peers,)), dma((peers,)), dma((peers,)), dma, dma,
         ],
         compiler_params=pltpu.CompilerParams(
-            collective_id=1, has_side_effects=True, vmem_limit_bytes=32 * 2**20),
+            collective_id=1, has_side_effects=True, vmem_limit_bytes=8 * 2**20),
     )(part)
 
 
@@ -389,59 +414,107 @@
     return hi, (x - hi.astype(jnp.float32)).astype(jnp.bfloat16)
 
 
-def invert(gram, size):
-    lane = lax.broadcasted_iota(jnp.int32, (8, size), 1)
-    sub = lax.broadcasted_iota(jnp.int32, (8, size), 0)
-    sub1 = lax.broadcasted_iota(jnp.int32, (8, 1), 0)
-    blocks = [gram[8 * t:8 * t + 8, :] + (lane == sub + 8 * t).astype(jnp.float32)
-              for t in range(size // 8)]
+def recip(x):
+    r = pl.reciprocal(x, approx=True)
+    return r * (2.0 - x * r)
+
+
+def tree_sum(terms):
+    while len(terms) > 1:
+        terms = [sum(terms[i:i + 2][1:], terms[i]) for i in range(0, len(terms), 2)]
+    return terms[0]
+
+
+def invert_block(x):
+    size, step = x.shape[0], 16
+    lane = lax.broadcasted_iota(jnp.int32, (step, size), 1)
+    sub = lax.broadcasted_iota(jnp.int32, (step, size), 0)
+    blocks = [x[i:i + step, :] for i in range(0, size, step)]
     done = []
-    for t in range(size // 8):
-        base = 8 * t
+    for t in range(size // step):
+        base = step * t
         row = blocks[t]
-        diag = [row[:, base + q:base + q + 1] for q in range(8)]
-        inv = jnp.zeros((8, 1), jnp.float32)
-        rsq = jnp.zeros((8, 1), jnp.float32)
-        for k in range(8):
-            pivot = diag[k][k:k + 1, :]
-            recip = 1.0 / pivot
-            inv = jnp.where(sub1 == k, recip, inv)
-            rsq = jnp.where(sub1 == k, lax.rsqrt(pivot), rsq)
-            if k < 7:
-                f = jnp.where(sub1 > k, diag[k] * recip, 0.0)
-                for q in range(k + 1, 8):
-                    diag[q] = diag[q] - f * diag[q][k:k + 1, :]
-                row = jnp.where((lane == base + k) & (sub > k), -f, row - f * row[k:k + 1, :])
-        inpanel = (lane >= base) & (lane < base + 8)
-        low = jnp.where(lane == base + sub, 1.0, jnp.where(lane > base + sub, 0.0, row))
-        done.append(low * rsq)
-        if t + 1 < size // 8:
-            used = jnp.where(inpanel, low, row)
-            factor = (row * inv).T
-            for s in range(t + 1, size // 8):
-                fac = factor[8 * s:8 * s + 8, :]
-                new = jnp.where(inpanel, 0.0, blocks[s])
-                for k in range(8):
-                    new = new - fac[:, k:k + 1] * used[k:k + 1, :]
-                blocks[s] = new
+        inpanel = (lane >= base) & (lane < base + step)
+        diag = [jnp.broadcast_to(row[:, base + q:base + q + 1], (step, size)) for q in range(step)]
+        aug = jnp.where(inpanel, jnp.where(lane == base + sub, 1.0, 0.0), row)
+        inv = jnp.zeros((step, size), jnp.float32)
+        piv = jnp.ones((step, size), jnp.float32)
+        for k in range(0, step, 2):
+            d0, d1 = diag[k], diag[k + 1]
+            a, b, c = d0[k:k + 1, :], d1[k:k + 1, :], d1[k + 1:k + 2, :]
+            det = a * c - b * b
+            ra, rdet = recip(a), recip(det)
+            ratio, rp = b * ra, a * rdet
+            inv = jnp.where(sub == k, ra, jnp.where(sub == k + 1, rp, inv))
+            piv = jnp.where(sub == k, a, jnp.where(sub == k + 1, det * ra, piv))
+            l0 = jnp.where(sub > k, d0 * ra, 0.0)
+            l1 = jnp.where(sub > k + 1, (d1 - l0 * b) * rp, 0.0)
+
+            def eliminate(z):
+                first = z[k:k + 1, :]
+                second = z[k + 1:k + 2, :] - ratio * first
+                return z - (l0 * first + l1 * second)
+
+            for q in range(k + 2, step):
+                diag[q] = eliminate(diag[q])
+            aug = eliminate(aug)
+        done.append(jnp.where(lane < base + step, aug, 0.0) * lax.rsqrt(piv))
+        if base + step < size:
+            factor = (aug * inv).T
+            for s in range(t + 1, size // step):
+                fac = factor[step * s:step * (s + 1), :]
+                terms = [fac[:, k:k + 1] * aug[k:k + 1, :] for k in range(step)]
+                blocks[s] = jnp.where(inpanel, 0.0, blocks[s]) - tree_sum(terms)
     return jnp.concatenate(done, axis=0)
 
 
-def mix_kernel(members, gram, fh, fu, fv, out, hi, lo):
-    @pl.when((pl.program_id(0) == 0) & (pl.program_id(1) == 0))
-    def _():
-        g = gram[...]
-        half = members // 2
-        proj = jnp.concatenate([g[members - 2:members - 1, :half], g[members - 1:members, :half]], axis=1)
-        inv = invert(gram, members)
-        part = jnp.sum(inv * proj, axis=1, keepdims=True)
-        weights = jnp.sum(inv * part, axis=0, keepdims=True)
-        t = inv + weights * (1.0 / math.sqrt(members - 1))
-        t = t + (1.0 - jnp.sum(t, axis=1, keepdims=True)) * (1.0 / members)
-        a, b = split(t)
-        hi[...] = a
-        lo[...] = b
-
+def dot_at(x, y, dims):
+    return lax.dot_general(x, y, (dims, ((), ())), precision=lax.Precision.HIGHEST,
+                           preferred_element_type=jnp.float32)
+
+
+def invert(gram):
+    size = gram.shape[0]
+    half = size // 2
+    i = lax.broadcasted_iota(jnp.int32, (half, half), 0)
+    j = lax.broadcasted_iota(jnp.int32, (half, half), 1)
+    eye = (i == j).astype(jnp.float32)
+    m1 = invert_block(gram[:half, :half] + eye)
+    side = dot_at(m1, gram[:half, half:], ((1,), (0,)))
+    st = side.T
+    m2 = invert_block(gram[half:, half:] + eye - dot_at(st, side, ((1,), (0,))))
+    low = -dot_at(m2, dot_at(st, m1, ((1,), (0,))), ((1,), (0,)))
+    top = jnp.concatenate([m1, jnp.zeros((half, half), jnp.float32)], axis=1)
+    return jnp.concatenate([top, jnp.concatenate([low, m2], axis=1)], axis=0)
+
+
+def factor_kernel(members, gram, hi, lo):
+    g = gram[...]
+    half = members // 2
+    proj = jnp.concatenate([g[members - 2:members - 1, :half], g[members - 1:members, :half]], axis=1)
+    inv = invert(g)
+    part = jnp.sum(inv * proj, axis=1, keepdims=True)
+    weights = jnp.sum(inv * part, axis=0, keepdims=True)
+    t = inv + weights * (1.0 / math.sqrt(members - 1))
+    t = t + (1.0 - jnp.sum(t, axis=1, keepdims=True)) * (1.0 / members)
+    a, b = split(t)
+    hi[...] = a
+    lo[...] = b
+
+
+def transform_of(gram):
+    members = gram.shape[0]
+    vmem = pl.BlockSpec(memory_space=pltpu.VMEM)
+    return pl.pallas_call(
+        functools.partial(factor_kernel, members),
+        out_shape=[jax.ShapeDtypeStruct((members, members), jnp.bfloat16)] * 2,
+        in_specs=[vmem],
+        out_specs=[vmem] * 2,
+        compiler_params=pltpu.CompilerParams(vmem_limit_bytes=12 * 2**20),
+    )(gram)
+
+
+def mix_kernel(members, hi, lo, fh, fu, fv, out):
     def mix(ref):
         dims = (((1,), (1,)), ((), ()))
         dot = functools.partial(lax.dot_general, dimension_numbers=dims, preferred_element_type=jnp.float32)
@@ -455,7 +528,7 @@
         pl.when(pl.program_id(0) == c)(functools.partial(mix, ref))
 
 
-def mixing(gram, fields):
+def mixing(hi, lo, fields):
     rows, cols, members = fields[0].shape
     width = 128
     steps = cols // width
@@ -467,18 +540,18 @@
         functools.partial(mix_kernel, members),
         grid=(3, steps),
         out_shape=jax.ShapeDtypeStruct((3, members * rows, cols), jnp.float32),
-        in_specs=[pl.BlockSpec((members, members), lambda i, j: (0, 0))] + [spec(c) for c in range(3)],
+        in_specs=[pl.BlockSpec((members, members), lambda i, j: (0, 0))] * 2 + [spec(c) for c in range(3)],
         out_specs=pl.BlockSpec((1, members * rows, width), lambda i, j: (i, 0, j)),
-        scratch_shapes=[pltpu.VMEM((members, members), jnp.bfloat16)] * 2,
-        compiler_params=pltpu.CompilerParams(vmem_limit_bytes=48 * 2**20),
-    )(gram, *fields)
+        compiler_params=pltpu.CompilerParams(vmem_limit_bytes=16 * 2**20),
+    )(hi, lo, *fields)
     return out.reshape(3, members, rows, cols)
 
 
 def shards(nlon, nlat, state, bathymetry, obs_index, obs_count, obs_value, obs_sd):
     h, u, v, part = forecast(nlon, nlat, state, bathymetry, obs_index, obs_count, obs_value, obs_sd)
     gram = total_sum(nlon, nlat, part)
-    return mixing(gram, (h, u, v))
+    hi, lo = transform_of(gram)
+    return mixing(hi, lo, (h, u, v))
 
 
 def solution(mesh):

time: 110 us -> 78.6 us (0.71)
  Pallas kernels: 103 us -> 70.1 us
  local copies, waits for them, and re-layouts: 5.9 us -> 7.49 us
    pallas_call x1, Pallas kernels: 49.7 us -> 7.67 us  [mixing(): pl.pallas_call(functools.partial(mix_kernel, members), grid=(3, steps), o...]
    pallas_call x0 -> x1, Pallas kernels: none -> 9.81 us  [transform_of(): pl.pallas_call(functools.partial(factor_kernel, members), out_shape=[jax....]
    unnamed x12 -> x14, local copies, waits for them, and re-layouts: 5.9 us -> 7.49 us
where the time goes in v2:
time: 78.6 us; the launch traced here: 78.3 us
  Pallas kernels  70.1 us (89%)
  local copies, waits for them, and re-layouts  7.49 us (10%)
    pallas_call x1, Pallas kernels, forecast(): pl.pallas_call(functools.partial(forecast_kernel, nlon, nlat, members, ro...  33.4 us
    pallas_call x1, Pallas kernels, total_sum(): pl.pallas_call(functools.partial(sum_kernel, nlon, nlat, size), out_shape...  19.2 us
    pallas_call x1, Pallas kernels, transform_of(): pl.pallas_call(functools.partial(factor_kernel, members), out_shape=[jax....  9.81 us
    pallas_call x1, Pallas kernels, mixing(): pl.pallas_call(functools.partial(mix_kernel, members), grid=(3, steps), o...  7.67 us
    unnamed x14, local copies, waits for them, and re-layouts  7.49 us

profile of v2, /device:TPU:0, one launch (start us, length us, event | category | flops | bytes accessed | tf_op | source)
XLA Modules:
  0.0 78.3 jit_solution(15017181584384787237)
XLA Ops:
  0.7 0.0 copy-start.3
  0.7 0.7 copy-done.3
  1.4 0.0 copy-start.4
  1.4 0.7 copy-done.4
  2.0 0.0 copy-start.5
  2.0 0.7 copy-done.5
  2.7 0.0 copy-start.6
  2.7 0.7 copy-done.6
  3.4 33.4 %shard_map.64 = (f32[8,256,256]{2,1,0:T(8,128)}, f32[8,256,256]{2,1,0:T(8,128)}, f32[8,256,256]{2,1,0:T(8,128)}, f32[256,256]{1,0:T(8,128)S(1)}) custom-call(f32[3,2048,256]{2,1,0:T(8,128)} %bitcast.8, f32[8,256]{1,0:T(8,128)S(1)} %copy-done.3, s32[1,256]{1,0:T(1,128)S(1)} %bitcast.5, s32[1,1]{1,0:T(1,128)S(6)} %copy.7.count_at, f32[1,256]{1,0:T(1,128)S(1)} %bitcast.6, ...), custom_call_target="tpu_custom_call" | custom-call | tf_op jit(solution)/shard_map/pallas_call | solution.py:248
  36.8 19.2 %shard_map.65.gram = f32[256,256]{1,0:T(8,128)S(1)} custom-call(f32[256,256]{1,0:T(8,128)S(1)} %get-tuple-element.11.part), custom_call_target="tpu_custom_call" | custom-call | tf_op jit(solution)/shard_map/pallas_call | solution.py:396
  56.0 9.8 %shard_map.66 = (bf16[256,256]{1,0:T(8,128)(2,1)S(1)}, bf16[256,256]{1,0:T(8,128)(2,1)S(1)}) custom-call(f32[256,256]{1,0:T(8,128)S(1)} %shard_map.65.gram), custom_call_target="tpu_custom_call" | custom-call | tf_op jit(solution)/shard_map/pallas_call | solution.py:508
  65.9 0.0 copy-start
  65.9 1.6 %copy-done = f32[8,256,256]{2,1,0:T(8,128)S(1)} copy-done((f32[8,256,256]{2,1,0:T(8,128)S(1)}, f32[8,256,256]{2,1,0:T(8,128)}, u32[]{:S(2)}) %copy-start) | copy-done | bytes 2097176
  67.4 0.0 copy-start.1
  67.4 1.6 %copy-done.1 = f32[8,256,256]{2,1,0:T(8,128)S(1)} copy-done((f32[8,256,256]{2,1,0:T(8,128)S(1)}, f32[8,256,256]{2,1,0:T(8,128)}, u32[]{:S(2)}) %copy-start.1) | copy-done | bytes 2097176
  69.0 0.0 copy-start.2
  69.0 1.6 %copy-done.2 = f32[8,256,256]{2,1,0:T(8,128)S(1)} copy-done((f32[8,256,256]{2,1,0:T(8,128)S(1)}, f32[8,256,256]{2,1,0:T(8,128)}, u32[]{:S(2)}) %copy-start.2) | copy-done | bytes 2097176
  70.6 7.7 %shard_map.67 = f32[3,2048,256]{2,1,0:T(8,128)} custom-call(bf16[256,256]{1,0:T(8,128)(2,1)S(1)} %get-tuple-element.12.hi, bf16[256,256]{1,0:T(8,128)(2,1)S(1)} %get-tuple-element.13.lo, f32[8,256,256]{2,1,0:T(8,128)S(1)} %copy-done, f32[8,256,256]{2,1,0:T(8,128)S(1)} %copy-done.1, f32[8,256,256]{2,1,0:T(8,128)S(1)} %copy-done.2), custom_call_target="tpu_custom_call" | custom-call | tf_op jit(solution)/shard_map/pallas_call | solution.py:539
Async XLA Ops:
  0.7 0.7 copy-start.3
  1.4 0.7 copy-start.4
  2.0 0.7 copy-start.5
  2.7 0.7 copy-start.6
  65.9 1.6 %copy-start = (f32[8,256,256]{2,1,0:T(8,128)S(1)}, f32[8,256,256]{2,1,0:T(8,128)}, u32[]{:S(2)}) copy-start(f32[8,256,256]{2,1,0:T(8,128)} %get-tuple-element.14.fh) | copy-start | bytes 6291460
  67.4 1.6 %copy-start.1 = (f32[8,256,256]{2,1,0:T(8,128)S(1)}, f32[8,256,256]{2,1,0:T(8,128)}, u32[]{:S(2)}) copy-start(f32[8,256,256]{2,1,0:T(8,128)} %get-tuple-element.15.fu) | copy-start | bytes 6291460
  69.0 1.6 %copy-start.2 = (f32[8,256,256]{2,1,0:T(8,128)S(1)}, f32[8,256,256]{2,1,0:T(8,128)}, u32[]{:S(2)}) copy-start(f32[8,256,256]{2,1,0:T(8,128)} %get-tuple-element.16.fv) | copy-start | bytes 6291460

commit v3 on v2

v3 whole, which is shorter than its diff:
```python
import functools
import math

import jax
import jax.numpy as jnp
from jax import lax
from jax.experimental import pallas as pl
from jax.experimental.pallas import tpu as pltpu
from jax.sharding import PartitionSpec as P

MESH = pl.DeviceIdType.MESH
PAD = 8


def forecast_kernel(nlon, nlat, members, rows, cols, state, bath_at, index_at, count_at, value_at, sd_at,
                    out_h, out_u, out_v, out, raw, hp, fu, fv, fxp, fy, brep, rbuf, csend, crecv, hx,
                    bath, index, count, value, sd, fc, part, other, acc, parts, whole, back,
                    lsem, isem, osem, rs, rr, cs, cr, ps, pr, ss, sr, gs, gr, qs, qr):
    lon, lat = lax.axis_index("lon"), lax.axis_index("lat")
    west, east = lax.rem(lon + nlon - 1, nlon), lax.rem(lon + 1, nlon)
    last = rows - 1
    has_n, has_s = lat > 0, lat < nlat - 1
    core, pair = lax.rem(lon, 2), lon // 2
    npair = nlon // 2
    peers = npair * nlat
    half = members // 2
    owners = min(peers, half // 8)
    chunk = half // owners
    me = lat * npair + pair
    partner = {"lon": lon + 1 - 2 * core}
    groups = members // 128
    tiles = cols // 128

    def device(p):
        return {"lon": 2 * lax.rem(p, npair) + core, "lat": p // npair}

    loads = [[pltpu.make_async_copy(state.at[c, :, pl.ds(128 * i, 128)], raw.at[c, i], lsem.at[c, i])
              for i in range(tiles)] for c in range(3)]
    small = [pltpu.make_async_copy(src, dst, isem.at[i]) for i, (src, dst) in enumerate((
        (bath_at, bath), (index_at, index), (count_at, count), (value_at, value), (sd_at, sd)))]
    small[0].start()
    for c in (2, 1, 0):
        for load in loads[c]:
            load.start()
    for load in small[1:]:
        load.start()
    barrier = pltpu.get_barrier_semaphore()
    pl.semaphore_signal(barrier, inc=1, device_id=partner, device_id_type=MESH)
    beyond = lax.rem(lon + nlon - 1 + 2 * core, nlon)
    pl.semaphore_signal(barrier, inc=1, device_id={"lon": beyond}, device_id_type=MESH)

    @pl.loop(1, peers)
    def _(d):
        pl.semaphore_signal(barrier, inc=1, device_id=device(lax.rem(me + d, peers)), device_id_type=MESH)

    small[0].wait()
    bt = bath[...].T
    for r in range(rows):
        brep[r] = jnp.broadcast_to(bt[:, r:r + 1], (cols, 128))
    at = (lat * rows + lax.broadcasted_iota(jnp.int32, (rows, 128), 0)).astype(jnp.float32)
    fc[...] = jnp.sin(math.pi / 3.0 * ((at + 0.5) / (rows * nlat) - 0.5))
    zero = jnp.zeros((cols, members), jnp.float32)

    @pl.when(jnp.logical_not(has_n))
    def _():
        for e in range(4):
            rbuf[e, 0] = zero

    @pl.when(jnp.logical_not(has_s))
    def _():
        for e in range(4):
            rbuf[e, 1] = zero

    def lanes(g):
        return pl.ds(128 * g, 128)

    def row_copy(e, g, north):
        if e % 2 == 0:
            src = fy.at[0 if north else last, :, lanes(g)]
        else:
            src = hp.at[0 if north else last, pl.ds(PAD, cols), lanes(g)]
        return pltpu.make_async_remote_copy(
            src_ref=src, dst_ref=rbuf.at[e, 1 if north else 0, :, lanes(g)],
            send_sem=rs.at[e, g, 0 if north else 1], recv_sem=rr.at[e, g, 1 if north else 0],
            device_id={"lat": lat - 1 if north else lat + 1}, device_id_type=MESH)

    def row_recv(e, g, side):
        here = rbuf.at[e, side, :, lanes(g)]
        return pltpu.make_async_remote_copy(
            src_ref=here, dst_ref=here, send_sem=rs.at[e, g, side], recv_sem=rr.at[e, g, side],
            device_id={"lat": lat - 1 if side == 0 else lat + 1}, device_id_type=MESH)

    def send_rows(e, g):
        @pl.when(has_n)
        def _():
            row_copy(e, g, True).start()

        @pl.when(has_s)
        def _():
            row_copy(e, g, False).start()

    def wait_rows(e, g):
        @pl.when(has_n)
        def _():
            row_copy(e, g, True).wait_send()
            row_recv(e, g, 0).wait_recv()

        @pl.when(has_s)
        def _():
            row_copy(e, g, False).wait_send()
            row_recv(e, g, 1).wait_recv()

    def col_copy(e, g, side):
        return pltpu.make_async_remote_copy(
            src_ref=csend.at[e, g, side], dst_ref=crecv.at[e, g, 1 - side],
            send_sem=cs.at[e, g, side], recv_sem=cr.at[e, g, 1 - side],
            device_id={"lon": west if side == 0 else east}, device_id_type=MESH)

    def send_cols(e, g, ref):
        for r in range(rows):
            csend[e, g, 0, r:r + 1, :] = ref[r, PAD:PAD + 1, lanes(g)]
            csend[e, g, 1, r:r + 1, :] = ref[r, PAD + cols - 1:PAD + cols, lanes(g)]
        col_copy(e, g, 0).start()
        col_copy(e, g, 1).start()

    def wait_cols(e, g, ref):
        for side in (0, 1):
            col_copy(e, g, side).wait()
        for r in range(rows):
            ref[r, PAD - 1:PAD, lanes(g)] = crecv[e, g, 0, r:r + 1, :]
            ref[r, PAD + cols:PAD + cols + 1, lanes(g)] = crecv[e, g, 1, r:r + 1, :]

    def slab(c, r, g):
        return jnp.concatenate(
            [raw[c, i, pl.ds(r + 128 * rows * g, 128, stride=rows), :].T for i in range(tiles)], axis=0)

    def dcol(ref, r, g):
        return ref[r, PAD + 1:PAD + cols + 1, lanes(g)] - ref[r, PAD - 1:PAD + cols - 1, lanes(g)]

    def hrow(r, g):
        return hp[r, PAD:PAD + cols, lanes(g)]

    def frow(r, g):
        return fy[r, :, lanes(g)]

    def load_v(r, g):
        v = slab(2, r, g)
        fv[r, :, lanes(g)] = v
        fy[r, :, lanes(g)] = v * brep[r]

    def height(r, g, up, down):
        div = dcol(fxp, r, g) + down - up
        hp[r, PAD:PAD + cols, lanes(g)] = hrow(r, g) - 0.25 * div

    def wind(r, g, up, down, flux):
        f = fc[pl.ds(r, 1), :]
        u, v = fu[r, :, lanes(g)], fv[r, :, lanes(g)]
        un = u + 0.5 * (f * v - 0.5 * dcol(hp, r, g))
        vn = v - 0.5 * (f * u + 0.5 * (down - up))
        fu[r, :, lanes(g)] = un
        fv[r, :, lanes(g)] = vn
        if flux:
            b = brep[r]
            fxp[r, PAD:PAD + cols, lanes(g)] = un * b
            fy[r, :, lanes(g)] = vn * b

    def edges_height(e, g):
        wait_rows(e, g)
        height(0, g, rbuf[e, 0, :, lanes(g)], frow(1, g))
        height(last, g, frow(last - 1, g), rbuf[e, 1, :, lanes(g)])
        send_rows(e + 1, g)

    def inner_height(g):
        @pl.loop(1, last)
        def _(r):
            height(r, g, frow(r - 1, g), frow(r + 1, g))

    def inner_wind(g, flux):
        @pl.loop(1, last)
        def _(r):
            wind(r, g, hrow(r - 1, g), hrow(r + 1, g), flux)

    def edges_wind(e, g, flux):
        wait_rows(e, g)
        wind(0, g, rbuf[e, 0, :, lanes(g)], hrow(1, g), flux)
        wind(last, g, hrow(last - 1, g), rbuf[e, 1, :, lanes(g)], flux)

    for load in loads[2]:
        load.wait()
    for g in range(groups):
        for r in (0, last):
            load_v(r, g)
        if g == 0:
            pl.semaphore_wait(barrier, peers + 1)
        send_rows(0, g)
    for load in loads[1]:
        load.wait()
    for g in range(groups):
        for r in range(rows):
            u = slab(1, r, g)
            fu[r, :, lanes(g)] = u
            fxp[r, PAD:PAD + cols, lanes(g)] = u * brep[r]
        send_cols(0, g, fxp)
        for r in range(1, last):
            load_v(r, g)
        if g == 0:
            for load in loads[0]:
                load.wait()
        for r in range(rows):
            hp[r, PAD:PAD + cols, lanes(g)] = slab(0, r, g)
        wait_cols(0, g, fxp)
        edges_height(0, g)
        inner_height(g)
        send_cols(1, g, hp)
    for g in range(groups):
        wait_cols(1, g, hp)
        inner_wind(g, True)
        edges_wind(1, g, True)
        send_rows(2, g)
        send_cols(2, g, fxp)
    for g in range(groups):
        wait_cols(2, g, fxp)
        inner_height(g)
        edges_height(2, g)
        send_cols(3, g, hp)

    out_copies = [
        pltpu.make_async_copy(hp.at[:, pl.ds(PAD, cols)], out_h, osem.at[0]),
        pltpu.make_async_copy(fu, out_u, osem.at[1]),
        pltpu.make_async_copy(fv, out_v, osem.at[2]),
    ]
    for load in small[1:]:
        load.wait()
    slots = hx.shape[0]

    @pl.loop(0, slots // 8)
    def _(t):
        got = []
        for k in range(8):
            cell = index[0, t * 8 + k]
            got.append(hp[cell // cols, pl.ds(PAD + lax.rem(cell, cols), 1), :])
        hx[pl.ds(t * 8, 8), :] = jnp.concatenate(got, axis=0)

    x = hx[...]
    info = jnp.concatenate([value[...], sd[...], jnp.zeros((6, slots), jnp.float32)], axis=0).T
    sigma = info[:, 1:2] * (math.sqrt(slots * nlon * nlat) / 16.0)
    valid = (lax.broadcasted_iota(jnp.int32, (slots, 1), 0) < count[0, 0]).astype(jnp.float32)
    mean = jnp.sum(x, axis=1, keepdims=True) * (1.0 / members)
    yp = (x - mean) * (valid / (math.sqrt(members - 1) * sigma))
    innov = (info[:, 0:1] - mean) * (valid / sigma)
    proj = jnp.sum(yp * innov, axis=0, keepdims=True)
    part[...] = jnp.dot(yp.T, yp, precision=lax.Precision.HIGHEST,
                        preferred_element_type=jnp.float32)
    part[members - 2:members - 1, 0:half] = proj[:, :half]
    part[members - 1:members, 0:half] = proj[:, half:]

    mine = pl.ds(pl.multiple_of(core * half, half), half)
    theirs = pl.ds(pl.multiple_of((1 - core) * half, half), half)

    def guard(cond, run):
        if owners == peers:
            run()
        else:
            pl.when(cond)(run)

    first = pltpu.make_async_remote_copy(
        src_ref=part.at[theirs], dst_ref=other, send_sem=ps, recv_sem=pr,
        device_id=partner, device_id_type=MESH)
    first.start()
    out_copies[0].start()
    first.wait()
    acc[...] = part[mine, :] + other[...]

    def scatter(p, frm):
        return pltpu.make_async_remote_copy(
            src_ref=acc.at[pl.ds(pl.multiple_of(p * chunk, chunk), chunk)], dst_ref=parts.at[frm],
            send_sem=ss.at[p], recv_sem=sr.at[frm], device_id=device(p), device_id_type=MESH)

    def arrive(frm):
        return pltpu.make_async_remote_copy(
            src_ref=parts.at[frm], dst_ref=parts.at[frm],
            send_sem=ss.at[0], recv_sem=sr.at[frm], device_id=device(frm), device_id_type=MESH)

    @pl.loop(1, peers)
    def _(d):
        p = lax.rem(me + d, peers)
        guard(p < owners, lambda: scatter(p, me).start())

    for g in range(groups):
        wait_cols(3, g, hp)
        inner_wind(g, False)

    def collect():
        total = acc[pl.ds(pl.multiple_of(me * chunk, chunk), chunk), :]

        def body(d, total):
            frm = lax.rem(me + d, peers)
            arrive(frm).wait_recv()
            return total + parts[frm]
        whole[me] = lax.fori_loop(1, peers, body, total)

    guard(me < owners, collect)

    def spread(p, frm):
        return pltpu.make_async_remote_copy(
            src_ref=whole.at[frm], dst_ref=whole.at[frm],
            send_sem=gs.at[p], recv_sem=gr.at[frm], device_id=device(p), device_id_type=MESH)

    def send_all():
        @pl.loop(1, peers)
        def _(d):
            p = lax.rem(me + d, peers)
            spread(p, me).start()

    guard(me < owners, send_all)
    for g in range(groups):
        edges_wind(3, g, False)
    out_copies[1].start()
    out_copies[2].start()

    @pl.loop(1, peers)
    def _(d):
        p = lax.rem(me + d, peers)
        guard(p < owners, lambda: spread(p, p).wait_recv())

    final = pltpu.make_async_remote_copy(
        src_ref=whole, dst_ref=back, send_sem=qs, recv_sem=qr,
        device_id=partner, device_id_type=MESH)
    final.start()

    @pl.loop(1, peers)
    def _(d):
        p = lax.rem(me + d, peers)
        guard(p < owners, lambda: scatter(p, me).wait_send())

    def sent_all():
        @pl.loop(1, peers)
        def _(d):
            p = lax.rem(me + d, peers)
            spread(p, me).wait_send()

    guard(me < owners, sent_all)
    out[mine, :] = whole[...].reshape(half, members)
    for copy in out_copies:
        copy.wait()
    final.wait()
    out[theirs, :] = back[...].reshape(half, members)


def forecast(nlon, nlat, state, bathymetry, obs_index, obs_count, obs_value, obs_sd):
    _, members, rows, cols = state.shape
    slots = obs_index.shape[2]
    f32, dma = jnp.float32, pltpu.SemaphoreType.DMA
    field = jax.ShapeDtypeStruct((rows, cols, members), f32)
    vmem, hbm = pl.BlockSpec(memory_space=pltpu.VMEM), pl.BlockSpec(memory_space=pltpu.HBM)
    half, peers, groups = members // 2, nlon // 2 * nlat, members // 128
    owners = min(peers, half // 8)
    chunk = half // owners
    return pl.pallas_call(
        functools.partial(forecast_kernel, nlon, nlat, members, rows, cols),
        out_shape=[field, field, field, jax.ShapeDtypeStruct((members, members), f32)],
        in_specs=[hbm] * 6,
        out_specs=[hbm] * 3 + [vmem],
        scratch_shapes=[
            pltpu.VMEM((3, cols // 128, members * rows, 128), f32),
            pltpu.VMEM((rows, cols + 2 * PAD, members), f32),
            pltpu.VMEM((rows, cols, members), f32),
            pltpu.VMEM((rows, cols, members), f32),
            pltpu.VMEM((rows, cols + 2 * PAD, members), f32),
            pltpu.VMEM((rows, cols, members), f32),
            pltpu.VMEM((rows, cols, 128), f32),
            pltpu.VMEM((4, 2, cols, members), f32),
            pltpu.VMEM((4, groups, 2, rows, 128), f32),
            pltpu.VMEM((4, groups, 2, rows, 128), f32),
            pltpu.VMEM((slots, members), f32),
            pltpu.VMEM((rows, cols), f32),
            pltpu.SMEM((1, slots), jnp.int32),
            pltpu.SMEM((1, 1), jnp.int32),
            pltpu.VMEM((1, slots), f32),
            pltpu.VMEM((1, slots), f32),
            pltpu.VMEM((rows, 128), f32),
            pltpu.VMEM((members, members), f32),
            pltpu.VMEM((half, members), f32), pltpu.VMEM((half, members), f32),
            pltpu.VMEM((peers, chunk, members), f32), pltpu.VMEM((owners, chunk, members), f32),
            pltpu.VMEM((owners, chunk, members), f32),
            dma((3, cols // 128)), dma((5,)), dma((3,)),
            dma((4, groups, 2)), dma((4, groups, 2)), dma((4, groups, 2)), dma((4, groups, 2)),
            dma, dma, dma((peers,)), dma((peers,)), dma((peers,)), dma((peers,)), dma, dma,
        ],
        compiler_params=pltpu.CompilerParams(
            collective_id=0, has_side_effects=True, vmem_limit_bytes=52 * 2**20),
    )(*(x if x.size == 1 else pltpu.with_memory_space_constraint(x, pltpu.HBM) for x in (
        state.reshape(3, members * rows, cols), bathymetry, obs_index.reshape(1, slots), obs_count,
        obs_value.reshape(1, slots), obs_sd.reshape(1, slots))))


def split(x):
    hi = x.astype(jnp.bfloat16)
    return hi, (x - hi.astype(jnp.float32)).astype(jnp.bfloat16)


def recip(x):
    r = pl.reciprocal(x, approx=True)
    return r * (2.0 - x * r)


def tree_sum(terms):
    while len(terms) > 1:
        terms = [sum(terms[i:i + 2][1:], terms[i]) for i in range(0, len(terms), 2)]
    return terms[0]


def invert_block(x):
    size, step = x.shape[0], 16
    lane = lax.broadcasted_iota(jnp.int32, (step, size), 1)
    sub = lax.broadcasted_iota(jnp.int32, (step, size), 0)
    blocks = [x[i:i + step, :] for i in range(0, size, step)]
    done = []
    for t in range(size // step):
        base = step * t
        row = blocks[t]
        inpanel = (lane >= base) & (lane < base + step)
        diag = [jnp.broadcast_to(row[:, base + q:base + q + 1], (step, size)) for q in range(step)]
        aug = jnp.where(inpanel, jnp.where(lane == base + sub, 1.0, 0.0), row)
        inv = jnp.zeros((step, size), jnp.float32)
        piv = jnp.ones((step, size), jnp.float32)
        for k in range(0, step, 2):
            d0, d1 = diag[k], diag[k + 1]
            a, b, c = d0[k:k + 1, :], d1[k:k + 1, :], d1[k + 1:k + 2, :]
            det = a * c - b * b
            ra, rdet = recip(a), recip(det)
            ratio, rp = b * ra, a * rdet
            inv = jnp.where(sub == k, ra, jnp.where(sub == k + 1, rp, inv))
            piv = jnp.where(sub == k, a, jnp.where(sub == k + 1, det * ra, piv))
            l0 = jnp.where(sub > k, d0 * ra, 0.0)
            l1 = jnp.where(sub > k + 1, (d1 - l0 * b) * rp, 0.0)

            def eliminate(z):
                first = z[k:k + 1, :]
                second = z[k + 1:k + 2, :] - ratio * first
                return z - (l0 * first + l1 * second)

            for q in range(k + 2, step):
                diag[q] = eliminate(diag[q])
            aug = eliminate(aug)
        done.append(jnp.where(lane < base + step, aug, 0.0) * lax.rsqrt(piv))
        if base + step < size:
            factor = (aug * inv).T
            for s in range(t + 1, size // step):
                fac = factor[step * s:step * (s + 1), :]
                terms = [fac[:, k:k + 1] * aug[k:k + 1, :] for k in range(step)]
                blocks[s] = jnp.where(inpanel, 0.0, blocks[s]) - tree_sum(terms)
    return jnp.concatenate(done, axis=0)


def dot_at(x, y, dims):
    return lax.dot_general(x, y, (dims, ((), ())), precision=lax.Precision.HIGHEST,
                           preferred_element_type=jnp.float32)


def invert(gram):
    size = gram.shape[0]
    half = size // 2
    i = lax.broadcasted_iota(jnp.int32, (half, half), 0)
    j = lax.broadcasted_iota(jnp.int32, (half, half), 1)
    eye = (i == j).astype(jnp.float32)
    m1 = invert_block(gram[:half, :half] + eye)
    side = dot_at(m1, gram[:half, half:], ((1,), (0,)))
    st = side.T
    m2 = invert_block(gram[half:, half:] + eye - dot_at(st, side, ((1,), (0,))))
    low = -dot_at(m2, dot_at(st, m1, ((1,), (0,))), ((1,), (0,)))
    top = jnp.concatenate([m1, jnp.zeros((half, half), jnp.float32)], axis=1)
    return jnp.concatenate([top, jnp.concatenate([low, m2], axis=1)], axis=0)


def factor_kernel(members, gram, hi, lo):
    g = gram[...]
    half = members // 2
    proj = jnp.concatenate([g[members - 2:members - 1, :half], g[members - 1:members, :half]], axis=1)
    inv = invert(g)
    part = jnp.sum(inv * proj, axis=1, keepdims=True)
    weights = jnp.sum(inv * part, axis=0, keepdims=True)
    t = inv + weights * (1.0 / math.sqrt(members - 1))
    t = t + (1.0 - jnp.sum(t, axis=1, keepdims=True)) * (1.0 / members)
    a, b = split(t)
    hi[...] = a
    lo[...] = b


def transform_of(gram):
    members = gram.shape[0]
    vmem = pl.BlockSpec(memory_space=pltpu.VMEM)
    return pl.pallas_call(
        functools.partial(factor_kernel, members),
        out_shape=[jax.ShapeDtypeStruct((members, members), jnp.bfloat16)] * 2,
        in_specs=[vmem],
        out_specs=[vmem] * 2,
        compiler_params=pltpu.CompilerParams(vmem_limit_bytes=12 * 2**20),
    )(gram)


def mix_kernel(members, hi, lo, fh, fu, fv, out):
    def mix(ref):
        dims = (((1,), (1,)), ((), ()))
        dot = functools.partial(lax.dot_general, dimension_numbers=dims, preferred_element_type=jnp.float32)
        rows = ref.shape[0]
        for r in range(rows):
            a, b = split(ref[r])
            out[0, pl.ds(r, members, stride=rows), :] = (
                dot(hi[...], a) + dot(hi[...], b) + dot(lo[...], a))

    for c, ref in enumerate((fh, fu, fv)):
        pl.when(pl.program_id(0) == c)(functools.partial(mix, ref))


def mixing(hi, lo, fields):
    rows, cols, members = fields[0].shape
    width = 128
    steps = cols // width

    def spec(c):
        return pl.BlockSpec((rows, width, members), lambda i, j: (0, jnp.where(i == c, j, jnp.where(i < c, 0, steps - 1)), 0))

    out = pl.pallas_call(
        functools.partial(mix_kernel, members),
        grid=(3, steps),
        out_shape=jax.ShapeDtypeStruct((3, members * rows, cols), jnp.float32),
        in_specs=[pl.BlockSpec((members, members), lambda i, j: (0, 0))] * 2 + [spec(c) for c in range(3)],
        out_specs=pl.BlockSpec((1, members * rows, width), lambda i, j: (i, 0, j)),
        compiler_params=pltpu.CompilerParams(vmem_limit_bytes=16 * 2**20),
    )(hi, lo, *fields)
    return out.reshape(3, members, rows, cols)


def shards(nlon, nlat, state, bathymetry, obs_index, obs_count, obs_value, obs_sd):
    h, u, v, gram = forecast(nlon, nlat, state, bathymetry, obs_index, obs_count, obs_value, obs_sd)
    h, u, v = (pltpu.with_memory_space_constraint(x, pltpu.HBM) for x in (h, u, v))
    hi, lo = transform_of(gram)
    return mixing(hi, lo, (h, u, v))


def solution(mesh):
    return jax.shard_map(
        functools.partial(shards, mesh.shape["lon"], mesh.shape["lat"]),
        mesh=mesh,
        in_specs=(
            P(None, None, "lat", "lon"),
            P("lat", "lon"),
            P("lat", "lon", None),
            P("lat", "lon"),
            P("lat", "lon", None),
            P("lat", "lon", None),
        ),
        out_specs=P(None, None, "lat", "lon"),
        check_vma=False,
    )
```

time: 78.6 us -> 64.6 us (0.82)
  local copies, waits for them, and re-layouts: 7.49 us -> 0 us
  Pallas kernels: 70.1 us -> 63.7 us
    pallas_call x1 -> x0, Pallas kernels: 19.2 us -> none  [total_sum(): pl.pallas_call(functools.partial(sum_kernel, nlon, nlat, size), out_shape...]
    pallas_call x1, Pallas kernels: 33.4 us -> 43.8 us  [forecast(): pl.pallas_call(functools.partial(forecast_kernel, nlon, nlat, members, ro...]
    unnamed x14 -> x0, local copies, waits for them, and re-layouts: 7.49 us -> none
    pallas_call x1, Pallas kernels: 7.67 us -> 10.2 us  [mixing(): pl.pallas_call(functools.partial(mix_kernel, members), grid=(3, steps), o...]
where the time goes in v3:
time: 64.6 us; the launch traced here: 64.4 us
  Pallas kernels  63.7 us (99%)
  between operations  0.67 us (1%)
    pallas_call x1, Pallas kernels, forecast(): pl.pallas_call(functools.partial(forecast_kernel, nlon, nlat, members, ro...  43.8 us
    pallas_call x1, Pallas kernels, mixing(): pl.pallas_call(functools.partial(mix_kernel, members), grid=(3, steps), o...  10.2 us
    pallas_call x1, Pallas kernels, transform_of(): pl.pallas_call(functools.partial(factor_kernel, members), out_shape=[jax....  9.81 us

profile of v3, /device:TPU:0, one launch (start us, length us, event | category | flops | bytes accessed | tf_op | source)
XLA Modules:
  0.0 64.4 jit_solution(2116559920654100978)
XLA Ops:
  0.7 43.8 %shard_map.64 = (f32[8,256,256]{2,1,0:T(8,128)}, f32[8,256,256]{2,1,0:T(8,128)}, f32[8,256,256]{2,1,0:T(8,128)}, f32[256,256]{1,0:T(8,128)S(1)}) custom-call(f32[3,2048,256]{2,1,0:T(8,128)} %bitcast.5, f32[8,256]{1,0:T(8,128)} %bath_at.1, s32[1,256]{1,0:T(1,128)} %bitcast.6, s32[1,1]{1,0:T(1,128)S(6)} %copy.7.count_at, f32[1,256]{1,0:T(1,128)} %bitcast.7, ...), custom_call_target="tpu_custom_call" | custom-call | tf_op jit(solution)/shard_map/pallas_call | solution.py:359
  44.4 9.8 %shard_map.65 = (bf16[256,256]{1,0:T(8,128)(2,1)S(1)}, bf16[256,256]{1,0:T(8,128)(2,1)S(1)}) custom-call(f32[256,256]{1,0:T(8,128)S(1)} %get-tuple-element.11.gram), custom_call_target="tpu_custom_call" | custom-call | tf_op jit(solution)/shard_map/pallas_call | solution.py:493
  54.2 10.2 %shard_map.66 = f32[3,2048,256]{2,1,0:T(8,128)} custom-call(bf16[256,256]{1,0:T(8,128)(2,1)S(1)} %get-tuple-element.12.hi, bf16[256,256]{1,0:T(8,128)(2,1)S(1)} %get-tuple-element.13.lo, f32[8,256,256]{2,1,0:T(8,128)} %get-tuple-element.14.fh, f32[8,256,256]{2,1,0:T(8,128)} %get-tuple-element.15.fu, f32[8,256,256]{2,1,0:T(8,128)} %get-tuple-element.16.fv), custom_call_target="tpu_custom_call" | custom-call | tf_op jit(solution)/shard_map/pallas_call | solution.py:524

commit v4 on v3

--- a/solution.py
+++ b/solution.py
@@ -13,9 +13,9 @@
 
 
 def forecast_kernel(nlon, nlat, members, rows, cols, state, bath_at, index_at, count_at, value_at, sd_at,
-                    out_h, out_u, out_v, out, raw, hp, fu, fv, fxp, fy, brep, rbuf, csend, crecv, hx,
+                    hp, fu, fv, out, raw, fxp, fy, brep, rbuf, csend, crecv, hx,
                     bath, index, count, value, sd, fc, part, other, acc, parts, whole, back,
-                    lsem, isem, osem, rs, rr, cs, cr, ps, pr, ss, sr, gs, gr, qs, qr):
+                    lsem, isem, rs, rr, cs, cr, ps, pr, ss, sr, gs, gr, qs, qr):
     lon, lat = lax.axis_index("lon"), lax.axis_index("lat")
     west, east = lax.rem(lon + nlon - 1, nlon), lax.rem(lon + 1, nlon)
     last = rows - 1
@@ -224,11 +224,6 @@
         edges_height(2, g)
         send_cols(3, g, hp)
 
-    out_copies = [
-        pltpu.make_async_copy(hp.at[:, pl.ds(PAD, cols)], out_h, osem.at[0]),
-        pltpu.make_async_copy(fu, out_u, osem.at[1]),
-        pltpu.make_async_copy(fv, out_v, osem.at[2]),
-    ]
     for load in small[1:]:
         load.wait()
     slots = hx.shape[0]
@@ -267,7 +262,6 @@
         src_ref=part.at[theirs], dst_ref=other, send_sem=ps, recv_sem=pr,
         device_id=partner, device_id_type=MESH)
     first.start()
-    out_copies[0].start()
     first.wait()
     acc[...] = part[mine, :] + other[...]
 
@@ -315,8 +309,6 @@
     guard(me < owners, send_all)
     for g in range(groups):
         edges_wind(3, g, False)
-    out_copies[1].start()
-    out_copies[2].start()
 
     @pl.loop(1, peers)
     def _(d):
@@ -341,8 +333,6 @@
 
     guard(me < owners, sent_all)
     out[mine, :] = whole[...].reshape(half, members)
-    for copy in out_copies:
-        copy.wait()
     final.wait()
     out[theirs, :] = back[...].reshape(half, members)
 
@@ -358,14 +348,11 @@
     chunk = half // owners
     return pl.pallas_call(
         functools.partial(forecast_kernel, nlon, nlat, members, rows, cols),
-        out_shape=[field, field, field, jax.ShapeDtypeStruct((members, members), f32)],
+        out_shape=[jax.ShapeDtypeStruct((rows, cols + 2 * PAD, members), f32), field, field, jax.ShapeDtypeStruct((members, members), f32)],
         in_specs=[hbm] * 6,
-        out_specs=[hbm] * 3 + [vmem],
+        out_specs=[vmem] * 4,
         scratch_shapes=[
             pltpu.VMEM((3, cols // 128, members * rows, 128), f32),
-            pltpu.VMEM((rows, cols + 2 * PAD, members), f32),
-            pltpu.VMEM((rows, cols, members), f32),
-            pltpu.VMEM((rows, cols, members), f32),
             pltpu.VMEM((rows, cols + 2 * PAD, members), f32),
             pltpu.VMEM((rows, cols, members), f32),
             pltpu.VMEM((rows, cols, 128), f32),
@@ -383,12 +370,12 @@
             pltpu.VMEM((half, members), f32), pltpu.VMEM((half, members), f32),
             pltpu.VMEM((peers, chunk, members), f32), pltpu.VMEM((owners, chunk, members), f32),
             pltpu.VMEM((owners, chunk, members), f32),
-            dma((3, cols // 128)), dma((5,)), dma((3,)),
+            dma((3, cols // 128)), dma((5,)),
             dma((4, groups, 2)), dma((4, groups, 2)), dma((4, groups, 2)), dma((4, groups, 2)),
             dma, dma, dma((peers,)), dma((peers,)), dma((peers,)), dma((peers,)), dma, dma,
         ],
         compiler_params=pltpu.CompilerParams(
-            collective_id=0, has_side_effects=True, vmem_limit_bytes=52 * 2**20),
+            collective_id=0, has_side_effects=True, vmem_limit_bytes=30 * 2**20),
     )(*(x if x.size == 1 else pltpu.with_memory_space_constraint(x, pltpu.HBM) for x in (
         state.reshape(3, members * rows, cols), bathymetry, obs_index.reshape(1, slots), obs_count,
         obs_value.reshape(1, slots), obs_sd.reshape(1, slots))))
@@ -473,7 +460,7 @@
     return jnp.concatenate([top, jnp.concatenate([low, m2], axis=1)], axis=0)
 
 
-def factor_kernel(members, gram, hi, lo):
+def analysis_kernel(members, gram, hp, fu, fv, out, hi, lo, buf, sem):
     g = gram[...]
     half = members // 2
     proj = jnp.concatenate([g[members - 2:members - 1, :half], g[members - 1:members, :half]], axis=1)
@@ -485,58 +472,47 @@
     a, b = split(t)
     hi[...] = a
     lo[...] = b
-
-
-def transform_of(gram):
-    members = gram.shape[0]
+    dims = (((1,), (1,)), ((), ()))
+    dot = functools.partial(lax.dot_general, dimension_numbers=dims, preferred_element_type=jnp.float32)
+    rows, cols, _ = fu.shape
+    copies = []
+    for c, ref in enumerate((hp, fu, fv)):
+        skip = PAD if c == 0 else 0
+        for i in range(cols // 128):
+            for r in range(0, rows, 2):
+                x = jnp.concatenate(
+                    [ref[r + k, skip + 128 * i:skip + 128 * (i + 1), :] for k in range(2)], axis=0)
+                a, b = split(x)
+                mixed = dot(hi[...], a) + dot(hi[...], b) + dot(lo[...], a)
+                for k in range(2):
+                    buf[c, i, pl.ds(r + k, members, stride=rows), :] = mixed[:, 128 * k:128 * (k + 1)]
+            copy = pltpu.make_async_copy(buf.at[c, i], out.at[c, :, pl.ds(128 * i, 128)], sem.at[c, i])
+            copy.start()
+            copies.append(copy)
+    for copy in copies:
+        copy.wait()
+
+
+def analyse(gram, fields):
+    rows, cols, members = fields[1].shape
+    tiles = cols // 128
     vmem = pl.BlockSpec(memory_space=pltpu.VMEM)
-    return pl.pallas_call(
-        functools.partial(factor_kernel, members),
-        out_shape=[jax.ShapeDtypeStruct((members, members), jnp.bfloat16)] * 2,
-        in_specs=[vmem],
-        out_specs=[vmem] * 2,
-        compiler_params=pltpu.CompilerParams(vmem_limit_bytes=12 * 2**20),
-    )(gram)
-
-
-def mix_kernel(members, hi, lo, fh, fu, fv, out):
-    def mix(ref):
-        dims = (((1,), (1,)), ((), ()))
-        dot = functools.partial(lax.dot_general, dimension_numbers=dims, preferred_element_type=jnp.float32)
-        rows = ref.shape[0]
-        for r in range(rows):
-            a, b = split(ref[r])
-            out[0, pl.ds(r, members, stride=rows), :] = (
-                dot(hi[...], a) + dot(hi[...], b) + dot(lo[...], a))
-
-    for c, ref in enumerate((fh, fu, fv)):
-        pl.when(pl.program_id(0) == c)(functools.partial(mix, ref))
-
-
-def mixing(hi, lo, fields):
-    rows, cols, members = fields[0].shape
-    width = 128
-    steps = cols // width
-
-    def spec(c):
-        return pl.BlockSpec((rows, width, members), lambda i, j: (0, jnp.where(i == c, j, jnp.where(i < c, 0, steps - 1)), 0))
-
     out = pl.pallas_call(
-        functools.partial(mix_kernel, members),
-        grid=(3, steps),
+        functools.partial(analysis_kernel, members),
         out_shape=jax.ShapeDtypeStruct((3, members * rows, cols), jnp.float32),
-        in_specs=[pl.BlockSpec((members, members), lambda i, j: (0, 0))] * 2 + [spec(c) for c in range(3)],
-        out_specs=pl.BlockSpec((1, members * rows, width), lambda i, j: (i, 0, j)),
-        compiler_params=pltpu.CompilerParams(vmem_limit_bytes=16 * 2**20),
-    )(hi, lo, *fields)
+        in_specs=[vmem] * 4,
+        out_specs=pl.BlockSpec(memory_space=pltpu.HBM),
+        scratch_shapes=[pltpu.VMEM((members, members), jnp.bfloat16)] * 2 + [
+            pltpu.VMEM((3, tiles, members * rows, 128), jnp.float32),
+            pltpu.SemaphoreType.DMA((3, tiles))],
+        compiler_params=pltpu.CompilerParams(vmem_limit_bytes=20 * 2**20),
+    )(gram, *fields)
     return out.reshape(3, members, rows, cols)
 
 
 def shards(nlon, nlat, state, bathymetry, obs_index, obs_count, obs_value, obs_sd):
     h, u, v, gram = forecast(nlon, nlat, state, bathymetry, obs_index, obs_count, obs_value, obs_sd)
-    h, u, v = (pltpu.with_memory_space_constraint(x, pltpu.HBM) for x in (h, u, v))
-    hi, lo = transform_of(gram)
-    return mixing(hi, lo, (h, u, v))
+    return analyse(gram, (h, u, v))
 
 
 def solution(mesh):

time: 64.6 us -> 57.9 us (0.90)
  Pallas kernels: 63.7 us -> 56.9 us
    pallas_call x2 -> x1, Pallas kernels: 20 us -> 13.1 us  [analyse(): pl.pallas_call(functools.partial(analysis_kernel, members), out_shape=jax...]
where the time goes in v4:
time: 57.9 us; the launch traced here: 57.7 us
  Pallas kernels  56.9 us (98%)
  between operations  0.82 us (1%)
    pallas_call x1, Pallas kernels, forecast(): pl.pallas_call(functools.partial(forecast_kernel, nlon, nlat, members, ro...  43.8 us
    pallas_call x1, Pallas kernels, analyse(): pl.pallas_call(functools.partial(analysis_kernel, members), out_shape=jax...  13.1 us

profile of v4, /device:TPU:0, one launch (start us, length us, event | category | flops | bytes accessed | tf_op | source)
XLA Modules:
  0.0 57.7 jit_solution(11580546086154638782)
XLA Ops:
  0.7 43.8 %shard_map.64 = (f32[8,272,256]{2,1,0:T(8,128)S(1)}, f32[8,256,256]{2,1,0:T(8,128)S(1)}, f32[8,256,256]{2,1,0:T(8,128)S(1)}, f32[256,256]{1,0:T(8,128)S(1)}) custom-call(f32[3,2048,256]{2,1,0:T(8,128)} %bitcast.5, f32[8,256]{1,0:T(8,128)} %bath_at.1, s32[1,256]{1,0:T(1,128)} %bitcast.6, s32[1,1]{1,0:T(1,128)S(6)} %copy.7.count_at, f32[1,256]{1,0:T(1,128)} %bitcast.7, ...), custom_call_target="tpu_custom_call" | custom-call | tf_op jit(solution)/shard_map/pallas_call | solution.py:349
  44.5 13.1 %shard_map.65 = f32[3,2048,256]{2,1,0:T(8,128)} custom-call(f32[256,256]{1,0:T(8,128)S(1)} %get-tuple-element.9.gram, f32[8,272,256]{2,1,0:T(8,128)S(1)} %get-tuple-element.10.hp, f32[8,256,256]{2,1,0:T(8,128)S(1)} %get-tuple-element.11.fu, f32[8,256,256]{2,1,0:T(8,128)S(1)} %get-tuple-element.12.fv), custom_call_target="tpu_custom_call" | custom-call | tf_op jit(solution)/shard_map/pallas_call | solution.py:500

commit v5 on v4

--- a/solution.py
+++ b/solution.py
@@ -14,7 +14,7 @@
 
 def forecast_kernel(nlon, nlat, members, rows, cols, state, bath_at, index_at, count_at, value_at, sd_at,
                     hp, fu, fv, out, raw, fxp, fy, brep, rbuf, csend, crecv, hx,
-                    bath, index, count, value, sd, fc, part, other, acc, parts, whole, back,
+                    bath, index, count, value, sd, fc, yt, part, other, acc, parts, whole, back,
                     lsem, isem, rs, rr, cs, cr, ps, pr, ss, sr, gs, gr, qs, qr):
     lon, lat = lax.axis_index("lon"), lax.axis_index("lat")
     west, east = lax.rem(lon + nlon - 1, nlon), lax.rem(lon + 1, nlon)
@@ -227,13 +227,18 @@
     for load in small[1:]:
         load.wait()
     slots = hx.shape[0]
+    bits = cols.bit_length() - 1
+    if cols == 1 << bits:
+        cell_row, cell_col = (lambda c: lax.shift_right_logical(c, bits)), (lambda c: c & (cols - 1))
+    else:
+        cell_row, cell_col = (lambda c: lax.div(c, cols)), (lambda c: lax.rem(c, cols))
 
     @pl.loop(0, slots // 8)
     def _(t):
         got = []
         for k in range(8):
             cell = index[0, t * 8 + k]
-            got.append(hp[cell // cols, pl.ds(PAD + lax.rem(cell, cols), 1), :])
+            got.append(hp[cell_row(cell), pl.ds(PAD + cell_col(cell), 1), :])
         hx[pl.ds(t * 8, 8), :] = jnp.concatenate(got, axis=0)
 
     x = hx[...]
@@ -244,10 +249,8 @@
     yp = (x - mean) * (valid / (math.sqrt(members - 1) * sigma))
     innov = (info[:, 0:1] - mean) * (valid / sigma)
     proj = jnp.sum(yp * innov, axis=0, keepdims=True)
-    part[...] = jnp.dot(yp.T, yp, precision=lax.Precision.HIGHEST,
-                        preferred_element_type=jnp.float32)
-    part[members - 2:members - 1, 0:half] = proj[:, :half]
-    part[members - 1:members, 0:half] = proj[:, half:]
+    hx[...] = yp
+    yt[...] = yp.T
 
     mine = pl.ds(pl.multiple_of(core * half, half), half)
     theirs = pl.ds(pl.multiple_of((1 - core) * half, half), half)
@@ -258,10 +261,22 @@
         else:
             pl.when(cond)(run)
 
+    def gram_rows(where):
+        part[where, :] = jnp.dot(yt[where, :], hx[...], precision=lax.Precision.HIGHEST,
+                                 preferred_element_type=jnp.float32)
+
+    def put_proj():
+        part[members - 2:members - 1, 0:half] = proj[:, :half]
+        part[members - 1:members, 0:half] = proj[:, half:]
+
     first = pltpu.make_async_remote_copy(
         src_ref=part.at[theirs], dst_ref=other, send_sem=ps, recv_sem=pr,
         device_id=partner, device_id_type=MESH)
+    gram_rows(theirs)
+    pl.when(core == 0)(put_proj)
     first.start()
+    gram_rows(mine)
+    pl.when(core == 1)(put_proj)
     first.wait()
     acc[...] = part[mine, :] + other[...]
 
@@ -283,6 +298,11 @@
     for g in range(groups):
         wait_cols(3, g, hp)
         inner_wind(g, False)
+
+    def forward(p):
+        return pltpu.make_async_remote_copy(
+            src_ref=whole.at[p], dst_ref=back.at[p], send_sem=qs.at[p], recv_sem=qr.at[p],
+            device_id=partner, device_id_type=MESH)
 
     def collect():
         total = acc[pl.ds(pl.multiple_of(me * chunk, chunk), chunk), :]
@@ -305,6 +325,7 @@
         def _(d):
             p = lax.rem(me + d, peers)
             spread(p, me).start()
+        forward(me).start()
 
     guard(me < owners, send_all)
     for g in range(groups):
@@ -313,12 +334,12 @@
     @pl.loop(1, peers)
     def _(d):
         p = lax.rem(me + d, peers)
-        guard(p < owners, lambda: spread(p, p).wait_recv())
-
-    final = pltpu.make_async_remote_copy(
-        src_ref=whole, dst_ref=back, send_sem=qs, recv_sem=qr,
-        device_id=partner, device_id_type=MESH)
-    final.start()
+
+        def relay():
+            spread(p, p).wait_recv()
+            forward(p).start()
+
+        guard(p < owners, relay)
 
     @pl.loop(1, peers)
     def _(d):
@@ -333,7 +354,11 @@
 
     guard(me < owners, sent_all)
     out[mine, :] = whole[...].reshape(half, members)
-    final.wait()
+
+    @pl.loop(0, owners)
+    def _(p):
+        forward(p).wait()
+
     out[theirs, :] = back[...].reshape(half, members)
 
 
@@ -366,13 +391,14 @@
             pltpu.VMEM((1, slots), f32),
             pltpu.VMEM((1, slots), f32),
             pltpu.VMEM((rows, 128), f32),
+            pltpu.VMEM((members, slots), f32),
             pltpu.VMEM((members, members), f32),
             pltpu.VMEM((half, members), f32), pltpu.VMEM((half, members), f32),
             pltpu.VMEM((peers, chunk, members), f32), pltpu.VMEM((owners, chunk, members), f32),
             pltpu.VMEM((owners, chunk, members), f32),
             dma((3, cols // 128)), dma((5,)),
             dma((4, groups, 2)), dma((4, groups, 2)), dma((4, groups, 2)), dma((4, groups, 2)),
-            dma, dma, dma((peers,)), dma((peers,)), dma((peers,)), dma((peers,)), dma, dma,
+            dma, dma, dma((peers,)), dma((peers,)), dma((peers,)), dma((peers,)), dma((owners,)), dma((owners,)),
         ],
         compiler_params=pltpu.CompilerParams(
             collective_id=0, has_side_effects=True, vmem_limit_bytes=30 * 2**20),

time: 57.9 us -> 57.1 us (0.986)
  Pallas kernels: 56.9 us -> 56.1 us
    pallas_call x1, Pallas kernels: 43.8 us -> 43 us  [forecast(): pl.pallas_call(functools.partial(forecast_kernel, nlon, nlat, members, ro...]
where the time goes in v5:
time: 57.1 us; the launch traced here: 56.9 us
  Pallas kernels  56.1 us (98%)
  between operations  0.82 us (1%)
    pallas_call x1, Pallas kernels, forecast(): pl.pallas_call(functools.partial(forecast_kernel, nlon, nlat, members, ro...  43 us
    pallas_call x1, Pallas kernels, analyse(): pl.pallas_call(functools.partial(analysis_kernel, members), out_shape=jax...  13.1 us

profile of v5, /device:TPU:0, one launch (start us, length us, event | category | flops | bytes accessed | tf_op | source)
XLA Modules:
  0.0 56.9 jit_solution(1454167304046054361)
XLA Ops:
  0.7 43.0 %shard_map.64 = (f32[8,272,256]{2,1,0:T(8,128)S(1)}, f32[8,256,256]{2,1,0:T(8,128)S(1)}, f32[8,256,256]{2,1,0:T(8,128)S(1)}, f32[256,256]{1,0:T(8,128)S(1)}) custom-call(f32[3,2048,256]{2,1,0:T(8,128)} %bitcast.5, f32[8,256]{1,0:T(8,128)} %bath_at.1, s32[1,256]{1,0:T(1,128)} %bitcast.6, s32[1,1]{1,0:T(1,128)S(6)} %copy.7.count_at, f32[1,256]{1,0:T(1,128)} %bitcast.7, ...), custom_call_target="tpu_custom_call" | custom-call | tf_op jit(solution)/shard_map/pallas_call | solution.py:374
  43.7 13.1 %shard_map.65 = f32[3,2048,256]{2,1,0:T(8,128)} custom-call(f32[256,256]{1,0:T(8,128)S(1)} %get-tuple-element.9.gram, f32[8,272,256]{2,1,0:T(8,128)S(1)} %get-tuple-element.10.hp, f32[8,256,256]{2,1,0:T(8,128)S(1)} %get-tuple-element.11.fu, f32[8,256,256]{2,1,0:T(8,128)S(1)} %get-tuple-element.12.fv), custom_call_target="tpu_custom_call" | custom-call | tf_op jit(solution)/shard_map/pallas_call | solution.py:526
